TPU v7x, 256 devices: a whole 4x4x8 slice. The times are simulated.
256 devices in a mesh: dp: 64 (over y, z, core), mp: 4 (over x).
Axes of the slice: x: 4, y: 4, z: 8, core: 2. Of those that a mesh axis runs over, the one named last changes fastest.
Arguments:
- documents: bfloat16 [131072, 1024], P('dp', 'mp'), may hold values from -6 to 6
- assign: int32 [131072], P('dp'), may hold values from 0 to 4095, as said below
- quality: float32 [131072], P('dp'), may hold values from 0.1 to 1
- centroids: bfloat16 [4096, 1024], P('mp'), may hold values from -6 to 6
Outputs:
- distances: float32 [131072], P('dp')
- new_centroids: bfloat16 [4096, 1024], P('dp', 'mp')
- cluster_quality: float32 [4096], P('dp')
- inertia: float32 [], replicated
Inputs may be any that keep to these rules, and one draw needn't show every extreme that they name: `assign`: call the clusters o * 64 to (o + 1) * 64 - 1 those of owner o. Among each run of 2048 documents held by one index of dp, at most 64 have clusters of any one owner, and one owner, the same for every index, gets exactly 64 of them from every index.
All inputs are finite; a program needn't handle non-finite values.
Results may differ from a plain program's by a relative error of at most 0.0044.
Values may be sent and summed in bfloat16 or wider, within the bound.
No kernel may reach another device: no remote copies, remote signals or barrier semaphores. Data moves between devices by JAX's collectives and lax.ppermute only.
A program may use at most 64 MiB of HBM per device.

v0:
```python
import jax
import jax.numpy as jnp
from jax import lax
from jax.sharding import PartitionSpec as P

D = 1024


def sent_to_all(shard, axis):
    copies = jnp.broadcast_to(shard, (lax.axis_size(axis), *shard.shape))
    return lax.all_to_all(copies, axis, split_axis=0, concat_axis=0, tiled=True)


def over_copies(shard, axis):
    return sent_to_all(shard, axis).sum(axis=0)


def per_device(documents, assign, quality, centroids):
    rows = documents.shape[0]
    width = documents.shape[1]
    feature_cents = lax.all_to_all(centroids, "mp", split_axis=1, concat_axis=0, tiled=True)
    clusters = feature_cents.shape[0]
    block = min(512, rows)
    labels = lax.broadcasted_iota(jnp.int32, (1, clusters), 1)
    weight_all = quality.astype(jnp.bfloat16)
    partial_list = []
    for start in range(0, rows, block):
        docs_blk = documents[start : start + block]
        onehot = (assign[start : start + block][:, None] == labels).astype(jnp.bfloat16)
        picked = jnp.dot(onehot, feature_cents, preferred_element_type=jnp.float32)
        diff = docs_blk.astype(jnp.float32) - picked
        partial_list.append(jnp.sum(diff * diff, axis=1))
    partial_value = jnp.concatenate(partial_list, axis=0)
    distances = over_copies(partial_value, "mp") / D
    total_docs = rows * lax.axis_size("dp")
    inertia = over_copies(jnp.sum(distances), "dp") / total_docs
    owners_count = lax.axis_size("dp")
    share = clusters // owners_count
    first = lax.axis_index("dp") * share
    capacity = max(2, 2 * rows // owners_count)
    owner_of = assign // share
    owner_hot = (owner_of[:, None] == lax.broadcasted_iota(jnp.int32, (1, owners_count), 1)).astype(
        jnp.int32
    )
    position = jnp.sum(jnp.cumsum(owner_hot, axis=0) * owner_hot, axis=1) - 1
    slot_index = owner_of * capacity + position
    send_docs = (
        jnp.zeros((owners_count * capacity, width), jnp.bfloat16).at[slot_index].set(documents)
    )
    send_weight = jnp.zeros((owners_count * capacity,), jnp.bfloat16).at[slot_index].set(weight_all)
    send_label = (
        jnp.full((owners_count * capacity,), -1, jnp.int32)
        .at[slot_index]
        .set(assign - owner_of * share)
    )
    recv_docs, recv_weight, recv_label = (
        lax.all_to_all(send_docs, "dp", split_axis=0, concat_axis=0, tiled=True),
        lax.all_to_all(send_weight, "dp", split_axis=0, concat_axis=0, tiled=True),
        lax.all_to_all(send_label, "dp", split_axis=0, concat_axis=0, tiled=True),
    )
    own_hot = (recv_label[:, None] == lax.broadcasted_iota(jnp.int32, (1, share), 1)).astype(
        jnp.bfloat16
    )
    own_weighted = own_hot * recv_weight[:, None]
    own_sums = lax.dot_general(
        own_weighted, recv_docs, (((0,), (0,)), ((), ())), preferred_element_type=jnp.float32
    )
    own_counts = jnp.sum(own_hot.astype(jnp.float32), axis=0)
    own_mass = jnp.sum(own_weighted.astype(jnp.float32), axis=0)
    old_rows = lax.dynamic_slice_in_dim(feature_cents, first, share, 0).astype(jnp.float32)
    new_centroids = ((own_sums + old_rows) / (own_mass + 1.0)[:, None]).astype(jnp.bfloat16)
    cluster_quality = own_mass / (own_counts + 1.0)
    return (distances, new_centroids, cluster_quality, inertia)


def solution(mesh):
    return jax.shard_map(
        per_device,
        mesh=mesh,
        in_specs=(P("dp", "mp"), P("dp"), P("dp"), P("mp", None)),
        out_specs=(P("dp"), P("dp", "mp"), P("dp"), P()),
        check_vma=False,
    )
```

profile of v0, /device:TPU:2, one launch (start us, length us, event | category | flops | bytes accessed | tf_op | source)
XLA Modules:
  0.0 188.3 jit_solution(15442149269551228526)
XLA Ops:
  0.6 3.1 %copy.60 = bf16[128,4,8,256]{3,2,0,1:T(8,128)(2,1)} copy(bf16[128,4,8,256]{3,2,1,0:T(8,128)(2,1)} %bitcast.34) | data formatting | bytes 4194304 | tf_op jit(solution)/shard_map/all_to_all | solution.py:21
  3.7 0.0 copy-start
  3.7 6.0 %all-to-all-start = ((bf16[1024,4,256]{2,0,1:T(8,128)(2,1)}), bf16[1024,4,256]{2,0,1:T(8,128)(2,1)S(1)}, u32[]{:S(2)}, u32[]{:S(2)}) async-start(bf16[1024,4,256]{2,0,1:T(8,128)(2,1)} %bitcast.32), calls=%async_computation | async-start | bytes 4194304 | tf_op jit(solution)/shard_map/all_to_all | solution.py:21
  9.7 0.0 copy-done
  9.7 0.0 copy-start.3
  9.7 0.9 fusion.42
  10.6 1.8 copy.55
  12.4 1.8 copy.54
  14.2 1.8 copy.53
  16.0 0.1 copy.52
  16.2 0.0 copy-done.3
  16.2 18.1 %reduce-window.6 = s32[64,16,128]{2,1,0:T(8,128)S(1)} reduce-window(s32[64,16,128]{2,1,0:T(8,128)S(1)} %fusion.30, s32[]{:T(128)} %constant.40.clone.1), window={size=1x1x128 pad=0_0x0_0x127_0}, to_apply=%region_5.0 | reduce-window | flops 16646144 | bytes 1048580 | tf_op jit(solution)/shard_map/reduce-window
  34.4 0.2 slice.40
  34.6 0.4 copy.49
  35.0 0.2 reduce-window.9
  35.2 0.2 broadcast_add_fusion
  35.4 0.2 fusion.28
  35.6 0.0 all-to-all-done
  35.6 0.0 copy-start.2
  35.7 3.1 %fusion.19 = f32[512]{0:T(512)S(1)} fusion(bf16[4096,256]{1,0:T(8,128)(2,1)S(1)} %bitcast.35, s32[512]{0:T(512)S(1)} %get-tuple-element.17, bf16[512,256]{0,1:T(8,128)(2,1)} %copy.55), kind=kOutput, calls=%fused_computation.27 | convolution fusion | flops 1076362752 | bytes 2363392 | tf_op jit(solution)/shard_map/dot_general | solution.py:30
  38.8 0.0 copy-done.2
  38.8 0.0 copy-start.1
  38.8 2.1 %fusion.18 = f32[512]{0:T(512)S(1)} fusion(bf16[4096,256]{1,0:T(8,128)(2,1)S(1)} %bitcast.36, s32[512]{0:T(512)S(1)} %get-tuple-element.18, bf16[512,256]{0,1:T(8,128)(2,1)S(1)} %copy-done.2), kind=kOutput, calls=%fused_computation.26 | convolution fusion | flops 1076362752 | bytes 2363392 | tf_op jit(solution)/shard_map/dot_general | solution.py:30
  41.0 0.0 copy-done.1
  41.0 2.1 %fusion.17 = f32[512]{0:T(512)S(1)} fusion(bf16[4096,256]{1,0:T(8,128)(2,1)S(1)} %bitcast.37, s32[512]{0:T(512)S(1)} %get-tuple-element.19, bf16[512,256]{0,1:T(8,128)(2,1)S(1)} %copy-done.1), kind=kOutput, calls=%fused_computation.25 | convolution fusion | flops 1076362752 | bytes 2363392 | tf_op jit(solution)/shard_map/dot_general | solution.py:30
  43.1 0.0 copy-start.4
  43.1 2.1 %fusion.16 = f32[512]{0:T(512)S(1)} fusion(bf16[4096,256]{1,0:T(8,128)(2,1)S(1)} %bitcast.38, s32[512]{0:T(512)S(1)} %get-tuple-element.16, bf16[512,256]{0,1:T(8,128)(2,1)S(1)} %copy.52), kind=kOutput, calls=%fused_computation.24 | convolution fusion | flops 1076362752 | bytes 2363392 | tf_op jit(solution)/shard_map/dot_general | solution.py:30
  45.3 0.6 broadcast_in_dim.12
  45.9 4.8 %all-to-all-start.1 = ((f32[4,1,2048]{2,1,0:T(1,128)}), f32[4,1,2048]{2,1,0:T(1,128)S(1)}, u32[]{:S(2)}, u32[]{:S(2)}) async-start(f32[4,1,2048]{2,1,0:T(1,128)} %broadcast_in_dim.12), calls=%async_computation.1 | async-start | bytes 65536 | tf_op jit(solution)/shard_map/all_to_all | solution.py:11
  50.7 0.0 copy-done.4
  50.8 14.6 %scatter_custom_fusion.1 = bf16[4096]{0:T(1024)(128)(2,1)S(1)} fusion(s32[2048]{0:T(1024)S(1)} %get-tuple-element.13, bf16[2048]{0:T(1024)(128)(2,1)S(1)} %convert_element_type.44, bf16[]{:T(256)} %constant.45.clone.1), kind=kCustom, calls=%fused_computation.60 | custom fusion | bytes 8194 | tf_op jit(solution)/shard_map/scatter | solution.py:50
  65.4 0.7 all_to_all.55
  66.0 0.0 all-to-all-done.1
  66.0 11.1 %all-to-all-start.3 = ((bf16[64,64,1]{1,2,0:T(2,128)(2,1)}), bf16[64,64,1]{1,2,0:T(2,128)(2,1)S(1)}, u32[]{:S(2)}, u32[]{:S(2)}) async-start(bf16[64,64,1]{1,2,0:T(2,128)(2,1)} %all_to_all.55), calls=%async_computation.3 | async-start | bytes 65536 | tf_op jit(solution)/shard_map/all_to_all | solution.py:58
  77.1 8.1 %scatter_custom_fusion = s32[4096]{0:T(1024)S(1)} fusion(s32[2048]{0:T(1024)S(1)} %get-tuple-element.13, s32[2048]{0:T(1024)S(1)} %get-tuple-element.12, s32[]{:T(128)} %constant.38.clone.1), kind=kCustom, calls=%fused_computation.56 | custom fusion | bytes 16388 | tf_op jit(solution)/shard_map/scatter | solution.py:54
  85.2 0.7 all_to_all.47
  85.9 0.7 all-to-all-done.3
  86.6 9.6 %all-to-all-start.2 = ((s32[64,64,1]{1,2,0:T(1,128)}), s32[64,64,1]{1,2,0:T(1,128)S(1)}, u32[]{:S(2)}, u32[]{:S(2)}) async-start(s32[64,64,1]{1,2,0:T(1,128)} %bitcast.7), calls=%async_computation.2 | async-start | bytes 65536 | tf_op jit(solution)/shard_map/all_to_all | solution.py:59
  96.3 1.2 fusion.41
  97.5 8.2 %all-to-all-done.2 = s32[64,64,1]{1,2,0:T(1,128)S(1)} async-done(((s32[64,64,1]{1,2,0:T(1,128)}), s32[64,64,1]{1,2,0:T(1,128)S(1)}, u32[]{:S(2)}, u32[]{:S(2)}) %all-to-all-start.2) | async-done | bytes 16416 | tf_op jit(solution)/shard_map/all_to_all | solution.py:59
  105.7 1.3 broadcast_in_dim.33
  107.0 4.6 %all-to-all-start.5 = ((f32[64,1,1]{2,1,0:T(1,128)}), f32[64,1,1]{2,1,0:T(1,128)S(1)}, u32[]{:S(2)}, u32[]{:S(2)}) async-start(f32[64,1,1]{2,1,0:T(1,128)} %broadcast_in_dim.33), calls=%async_computation.5 | async-start | bytes 65536 | tf_op jit(solution)/shard_map/all_to_all | solution.py:11
  111.6 11.2 %scatter_custom_fusion.2 = bf16[4096,256]{1,0:T(8,128)(2,1)} fusion(s32[2048]{0:T(1024)S(1)} %get-tuple-element.13, bf16[2048,256]{1,0:T(8,128)(2,1)} %param.4, bf16[]{:T(256)} %constant.45.clone.1), kind=kCustom, calls=%fused_computation.33 | custom fusion | bytes 2097664 | tf_op jit(solution)/shard_map/scatter | solution.py:48
  122.8 0.0 all-to-all-done.5
  122.8 10.6 %all-to-all-start.4 = ((bf16[64,64,256]{2,1,0:T(8,128)(2,1)}), bf16[64,64,256]{2,1,0:T(8,128)(2,1)}, u32[]{:S(2)}, u32[]{:S(2)}) async-start(bf16[64,64,256]{2,1,0:T(8,128)(2,1)} %bitcast.8), calls=%async_computation.4 | async-start | bytes 4194304 | tf_op jit(solution)/shard_map/all_to_all | solution.py:57
  133.4 0.1 reduce.3
  133.5 0.1 mul.38
  133.6 0.5 broadcast.86
  134.1 0.7 reduce.6
  134.8 0.1 eq.109
  134.9 0.4 convert_reduce_fusion
  135.3 0.5 add_divide_fusion
  135.8 0.7 reduce_sum.99
  137.1 47.3 %all-to-all-done.4 = bf16[64,64,256]{2,1,0:T(8,128)(2,1)} async-done(((bf16[64,64,256]{2,1,0:T(8,128)(2,1)}), bf16[64,64,256]{2,1,0:T(8,128)(2,1)}, u32[]{:S(2)}, u32[]{:S(2)}) %all-to-all-start.4) | async-done | bytes 2097184 | tf_op jit(solution)/shard_map/all_to_all | solution.py:57
  184.4 2.7 %fusion.21 = bf16[64,256]{1,0:T(8,128)(2,1)} fusion(bf16[4096,256]{1,0:T(8,128)(2,1)} %bitcast.9, s32[4096]{0:T(1024)S(1)} %eq.109, bf16[4096]{0:T(1024)(128)(2,1)S(1)} %mul.38, f32[64]{0:T(128)S(1)} %get-tuple-element.21, bf16[4096,256]{1,0:T(8,128)(2,1)S(1)} %bitcast.39, s32[]{:T(128)S(6)} %select_n.15), kind=kOutput, calls=%fused_computation.30 | convolution fusion | flops 134807552 | bytes 2187524 | tf_op jit(solution)/shard_map/dot_general | solution.py:65
  (7 shorter events, 0.1 us)
Async XLA Ops:
  3.7 6.0 %copy-start = (bf16[2048,256]{1,0:T(8,128)(2,1)S(1)}, bf16[2048,256]{1,0:T(8,128)(2,1)}, u32[]{:S(2)}) copy-start(bf16[2048,256]{1,0:T(8,128)(2,1)} %param.4) | copy-start | bytes 3145732
  3.7 31.9 %all-to-all-start = ((bf16[1024,4,256]{2,0,1:T(8,128)(2,1)}), bf16[1024,4,256]{2,0,1:T(8,128)(2,1)S(1)}, u32[]{:S(2)}, u32[]{:S(2)}) async-start(bf16[1024,4,256]{2,0,1:T(8,128)(2,1)} %bitcast.32), calls=%async_computation | async-start | bytes 4194304 | tf_op jit(solution)/shard_map/all_to_all | solution.py:21
  9.7 6.5 %copy-start.3 = (s32[2048]{0:T(1024)S(1)}, s32[2048]{0:T(1024)}, u32[]{:S(2)}) copy-start(s32[2048]{0:T(1024)} %param.5) | copy-start | bytes 24580
  35.6 3.1 %copy-start.2 = (bf16[512,256]{0,1:T(8,128)(2,1)S(1)}, bf16[512,256]{0,1:T(8,128)(2,1)}, u32[]{:S(2)}) copy-start(bf16[512,256]{0,1:T(8,128)(2,1)} %copy.54) | copy-start | bytes 786436
  38.8 2.2 %copy-start.1 = (bf16[512,256]{0,1:T(8,128)(2,1)S(1)}, bf16[512,256]{0,1:T(8,128)(2,1)}, u32[]{:S(2)}) copy-start(bf16[512,256]{0,1:T(8,128)(2,1)} %copy.53) | copy-start | bytes 786436
  43.1 7.6 %copy-start.4 = (f32[2048]{0:T(1024)S(1)}, f32[2048]{0:T(1024)}, u32[]{:S(2)}) copy-start(f32[2048]{0:T(1024)} %param.6) | copy-start | bytes 24580
  45.9 20.1 %all-to-all-start.1 = ((f32[4,1,2048]{2,1,0:T(1,128)}), f32[4,1,2048]{2,1,0:T(1,128)S(1)}, u32[]{:S(2)}, u32[]{:S(2)}) async-start(f32[4,1,2048]{2,1,0:T(1,128)} %broadcast_in_dim.12), calls=%async_computation.1 | async-start | bytes 65536 | tf_op jit(solution)/shard_map/all_to_all | solution.py:11
  66.0 20.6 %all-to-all-start.3 = ((bf16[64,64,1]{1,2,0:T(2,128)(2,1)}), bf16[64,64,1]{1,2,0:T(2,128)(2,1)S(1)}, u32[]{:S(2)}, u32[]{:S(2)}) async-start(bf16[64,64,1]{1,2,0:T(2,128)(2,1)} %all_to_all.55), calls=%async_computation.3 | async-start | bytes 65536 | tf_op jit(solution)/shard_map/all_to_all | solution.py:58
  86.6 19.1 %all-to-all-start.2 = ((s32[64,64,1]{1,2,0:T(1,128)}), s32[64,64,1]{1,2,0:T(1,128)S(1)}, u32[]{:S(2)}, u32[]{:S(2)}) async-start(s32[64,64,1]{1,2,0:T(1,128)} %bitcast.7), calls=%async_computation.2 | async-start | bytes 65536 | tf_op jit(solution)/shard_map/all_to_all | solution.py:59
  107.0 15.8 %all-to-all-start.5 = ((f32[64,1,1]{2,1,0:T(1,128)}), f32[64,1,1]{2,1,0:T(1,128)S(1)}, u32[]{:S(2)}, u32[]{:S(2)}) async-start(f32[64,1,1]{2,1,0:T(1,128)} %broadcast_in_dim.33), calls=%async_computation.5 | async-start | bytes 65536 | tf_op jit(solution)/shard_map/all_to_all | solution.py:11
  122.8 61.6 %all-to-all-start.4 = ((bf16[64,64,256]{2,1,0:T(8,128)(2,1)}), bf16[64,64,256]{2,1,0:T(8,128)(2,1)}, u32[]{:S(2)}, u32[]{:S(2)}) async-start(bf16[64,64,256]{2,1,0:T(8,128)(2,1)} %bitcast.8), calls=%async_computation.4 | async-start | bytes 4194304 | tf_op jit(solution)/shard_map/all_to_all | solution.py:57
where the time goes:
time: 190 us; the launch traced here: 188 us
  waiting for transfers between devices  56.2 us (30%)
  local copies, waits for them, and re-layouts  48 us (25%)
  starting transfers between devices  46.7 us (25%)
  other arithmetic  22.4 us (12%)
  matrix products  12.2 us (6%)
  between operations  2.62 us (1%)
    all_to_all x1, waiting for transfers between devices, per_device(): lax.all_to_all(send_docs, 'dp', split_axis=0, concat_axis=0, tiled=True)  47.3 us
    another operation x3, other arithmetic  18.5 us
    scatter x1, local copies, waits for them, and re-layouts, per_device(): jnp.zeros((owners_count * capacity,), jnp.bfloat16).at[slot_index]  14.6 us
    scatter x1, local copies, waits for them, and re-layouts, per_device(): jnp.zeros((owners_count * capacity, width), jnp.bfloat16).at[slot_index]  11.2 us
    all_to_all x1, starting transfers between devices, per_device(): lax.all_to_all(send_weight, 'dp', split_axis=0, concat_axis=0, tiled=True)  11.1 us
    all_to_all x1, starting transfers between devices, per_device(): lax.all_to_all(send_docs, 'dp', split_axis=0, concat_axis=0, tiled=True)  10.6 us
    all_to_all x1, starting transfers between devices, per_device(): lax.all_to_all(send_label, 'dp', split_axis=0, concat_axis=0, tiled=True)  9.64 us
    dot_general x4, matrix products, per_device(): picked = jnp.dot(onehot, feature_cents, preferred_element_type=jnp.float32)  9.56 us
  transfers between devices with their start and end apart: 6, of which 3 were waited for; matrix products, arithmetic and copies ran while one was open for 34% of the time, Pallas kernels for 0%

commit v1 on v0

v1 whole, which is shorter than its diff:
```python
import jax
import jax.numpy as jnp
from jax import lax
from jax.experimental import pallas as pl
from jax.experimental.pallas import tpu as pltpu
from jax.sharding import Mesh, PartitionSpec as P

D = 1024
F32 = jnp.float32
BF16 = jnp.bfloat16
TILE = 256
LANES = 128


def all_to_all(x, axes):
    return lax.all_to_all(x, axes, split_axis=0, concat_axis=0, tiled=True)


def scatter_kernel(own_aux, own_docs, oth_aux, oth_docs, sums, hist):
    rows = own_docs.shape[0]
    tiles = sums.shape[0] // TILE
    sub = lax.broadcasted_iota(jnp.int32, (TILE, LANES), 0).astype(F32).astype(BF16)
    sides = ((own_aux, own_docs), (oth_aux, oth_docs))

    def cluster_tile(t, carry):
        total = jnp.zeros((TILE, own_docs.shape[1]), F32)
        base = (t * TILE).astype(F32)
        for aux, docs in sides:
            rel = jnp.clip(aux[0] - base, -1.0, float(TILE)).astype(BF16)
            weight = aux[1].astype(BF16)
            hot = jnp.concatenate(
                [
                    jnp.where(
                        sub == jnp.broadcast_to(rel[r : r + 1], (TILE, LANES)),
                        jnp.broadcast_to(weight[r : r + 1], (TILE, LANES)),
                        jnp.zeros((TILE, LANES), BF16),
                    )
                    for r in range(rows // LANES)
                ],
                axis=1,
            )
            total = total + jnp.dot(hot, docs[...], preferred_element_type=F32)
        sums[pl.ds(pl.multiple_of(t * TILE, TILE), TILE), :] = total.astype(BF16)
        return carry

    lax.fori_loop(0, tiles, cluster_tile, 0)

    owners = hist.shape[0]
    share = hist.shape[1] // 2
    owner_sub = lax.broadcasted_iota(jnp.int32, (owners, LANES), 0).astype(F32)
    local_sub = lax.broadcasted_iota(jnp.int32, (share, LANES), 0).astype(F32)
    total = jnp.zeros(hist.shape, F32)
    for aux, docs in sides:
        label = aux[0]
        owner = jnp.floor(label * (1.0 / share))
        local = label - owner * share
        weight = aux[1]
        owner_hot, local_hot = [], []
        for r in range(rows // LANES):
            owner_hot.append((owner_sub == owner[r : r + 1]).astype(F32))
            same = local_sub == local[r : r + 1]
            local_hot.append(
                jnp.concatenate(
                    [same.astype(F32), jnp.where(same, weight[r : r + 1], 0.0)], axis=0
                )
            )
        total = total + lax.dot_general(
            jnp.concatenate(owner_hot, axis=1).astype(BF16),
            jnp.concatenate(local_hot, axis=1).astype(BF16),
            (((1,), (1,)), ((), ())),
            preferred_element_type=F32,
        )
    hist[...] = total


def distance_kernel(core, own_aux, own_docs, oth_aux, oth_docs, table, out):
    rows = own_docs.shape[0]
    clusters = table.shape[0]
    lane = lax.broadcasted_iota(jnp.int32, (TILE, TILE), 1).astype(F32).astype(BF16)
    me = core[0]
    per = TILE // LANES
    total = jnp.zeros((1, LANES), F32)
    for side, (aux, docs) in enumerate(((own_aux, own_docs), (oth_aux, oth_docs))):
        where_to = me if side == 0 else 1 - me

        def doc_tile(i, total):
            columns = []
            for j in range(per):
                label = aux[0, pl.ds(i * per + j, 1), :]
                columns.append(jnp.broadcast_to(label, (LANES, LANES)).T)
            column = jnp.concatenate(columns, axis=0)
            high = jnp.floor(column * (1.0 / TILE))
            low = (column - high * TILE).astype(BF16)
            high = high.astype(BF16)
            same = jnp.concatenate([low, low], axis=1) == lane
            hots = []
            for t in range(clusters // TILE):
                hit = jnp.where(
                    high == jnp.full((TILE, LANES), t, BF16),
                    jnp.ones((TILE, LANES), BF16),
                    jnp.zeros((TILE, LANES), BF16),
                )
                hots.append(
                    jnp.where(
                        same, jnp.concatenate([hit, hit], axis=1), jnp.zeros((TILE, TILE), BF16)
                    )
                )
            hot = jnp.concatenate(hots, axis=1)
            picked = jnp.dot(hot, table[...], preferred_element_type=F32)
            start = pl.multiple_of(i * TILE, TILE)
            diff = docs[pl.ds(start, TILE), :].astype(F32) - picked
            square = diff * diff
            folded = square[:, :LANES]
            for k in range(1, square.shape[1] // LANES):
                folded = folded + square[:, k * LANES : (k + 1) * LANES]
            for j in range(per):
                row = jnp.sum(folded[j * LANES : (j + 1) * LANES].T, axis=0, keepdims=True)
                row = jnp.where(aux[0, pl.ds(i * per + j, 1), :] >= 0.0, row, 0.0)
                out[where_to, 0, pl.ds(i * per + j, 1), :] = row
                total = total + row
            return total

        total = lax.fori_loop(0, rows // TILE, doc_tile, total)
    docs_rows = rows // LANES
    for c in range(2):
        out[c, 0, pl.ds(docs_rows, out.shape[2] - docs_rows), :] = jnp.broadcast_to(
            total, (out.shape[2] - docs_rows, LANES)
        )
    for c in range(2):
        for m in range(1, out.shape[1]):
            out[c, m] = out[c, 0]


def update_kernel(recv, tail, old, centroids, quality, inertia):
    share = old.shape[0]
    totals = jnp.sum(tail[...], axis=0)
    counts = totals[0:1, 0:share]
    mass = totals[0:1, share : 2 * share]
    quality[...] = mass / (counts + 1.0)
    inertia[...] = jnp.broadcast_to(
        jnp.sum(totals[1:2, :], axis=1, keepdims=True), inertia.shape
    )
    sums = recv[0].astype(F32)
    for p in range(1, recv.shape[0]):
        sums = sums + recv[p].astype(F32)
    wide = jnp.broadcast_to(totals[0:1, :], (LANES, LANES)).T[share : 2 * share]
    divisor = jnp.concatenate([wide] * (old.shape[1] // LANES), axis=1) + 1.0
    centroids[...] = ((sums + old[...].astype(F32)) / divisor).astype(BF16)


def per_device(documents, assign, quality, centroids):
    rows, width = documents.shape
    core = lax.axis_index("c")
    n_mp = lax.axis_size("mp")
    n_yz = lax.axis_size("y") * lax.axis_size("z")
    clusters = centroids.shape[0] * n_mp
    share = clusters // (2 * n_yz)
    half = clusters // 2
    groups = rows // LANES
    params = pltpu.CompilerParams(vmem_limit_bytes=32 * 1024 * 1024)

    oth_docs = lax.ppermute(documents, "c", [(0, 1), (1, 0)])
    owner = assign // share
    label = (owner // 2) * share + assign % share
    weight = quality.astype(BF16).astype(F32).reshape(groups, LANES)
    own_label = jnp.where(owner % 2 == core, label, -1).astype(F32).reshape(groups, LANES)
    oth_label = jnp.where(owner % 2 == core, -1, label).astype(F32).reshape(groups, LANES)
    own_aux = jnp.stack([own_label, weight])
    oth_aux = lax.ppermute(jnp.stack([oth_label, weight]), "c", [(0, 1), (1, 0)])

    block = centroids.reshape(-1, 2, share, n_mp, width)
    block = lax.dynamic_index_in_dim(block, core, 1, keepdims=False)
    block = block.transpose(2, 0, 1, 3).reshape(n_mp, half // n_mp, width)
    table = all_to_all(block, "mp").reshape(half, width)

    sums, hist = pl.pallas_call(
        scatter_kernel,
        out_shape=(
            jax.ShapeDtypeStruct((half, width), BF16),
            jax.ShapeDtypeStruct((n_yz, 2 * share), F32),
        ),
        compiler_params=params,
        cost_estimate=pl.CostEstimate(
            flops=4 * rows * half * width, bytes_accessed=3 * rows * width * 2, transcendentals=0
        ),
        name="scatter",
    )(own_aux, documents, oth_aux, oth_docs)
    recv = all_to_all(sums.reshape(n_yz, share, width), ("y", "z"))

    pieces = pl.pallas_call(
        distance_kernel,
        out_shape=jax.ShapeDtypeStruct((2, n_mp, groups + 8, LANES), F32),
        in_specs=[pl.BlockSpec(memory_space=pltpu.SMEM)]
        + [pl.BlockSpec(memory_space=pltpu.VMEM)] * 5,
        compiler_params=params,
        cost_estimate=pl.CostEstimate(
            flops=4 * rows * half * width, bytes_accessed=3 * rows * width * 2, transcendentals=0
        ),
        name="distances",
    )(core.astype(jnp.int32).reshape(1), own_aux, documents, oth_aux, oth_docs, table)
    arrived = all_to_all(pieces.reshape(2 * n_mp, groups + 8, LANES), ("c", "mp"))
    arrived = jnp.sum(arrived, axis=0)
    distances = (arrived[:groups] / D).reshape(rows)

    total_docs = rows * n_yz * 2
    row = arrived[groups : groups + 1] / D / total_docs
    tail = jnp.concatenate(
        [hist.reshape(n_yz, 1, LANES), jnp.broadcast_to(row[None], (n_yz, 1, LANES))], axis=1
    )
    tail = jnp.pad(tail, ((0, 0), (0, 6), (0, 0)))
    tail = all_to_all(tail, ("y", "z"))

    first = (lax.axis_index("y") * lax.axis_size("z") + lax.axis_index("z")) * share
    old = lax.dynamic_slice_in_dim(table, first, share, 0)
    new_centroids, cluster_quality, inertia = pl.pallas_call(
        update_kernel,
        out_shape=(
            jax.ShapeDtypeStruct((share, width), BF16),
            jax.ShapeDtypeStruct((1, share), F32),
            jax.ShapeDtypeStruct((1, LANES), F32),
        ),
        compiler_params=params,
        name="update",
    )(recv, tail, old)
    return distances, new_centroids, cluster_quality.reshape(share), inertia[0, 0]


def solution(mesh):
    n_dp, n_mp = mesh.devices.shape
    n_y, n_z = 4, n_dp // 8
    fine = Mesh(mesh.devices.reshape(n_y, n_z, 2, n_mp), ("y", "z", "c", "mp"))
    dp = ("y", "z", "c")
    return jax.shard_map(
        per_device,
        mesh=fine,
        in_specs=(P(dp, "mp"), P(dp), P(dp), P("mp", None)),
        out_specs=(P(dp), P(dp, "mp"), P(dp), P()),
        check_vma=False,
    )
```

time: 190 us -> 104 us (0.55)
  local copies, waits for them, and re-layouts: 48 us -> 4.93 us
  starting transfers between devices: 46.7 us -> 14.8 us
  other arithmetic: 22.4 us -> 0.69 us
  blocking collectives: 0 us -> 20.7 us
  Pallas kernels: 0 us -> 20.1 us
  waiting for transfers between devices: 56.2 us -> 41.7 us
  matrix products: 12.2 us -> 0 us
    scatter x3 -> x0, local copies, waits for them, and re-layouts: 33.9 us -> none  [the longest x1 14.6 us: per_device(): jnp.zeros((owners_count * capacity,), jnp.bfloat16).at[slot_index]]
    all_to_all x6 -> x3, starting transfers between devices: 46.7 us -> 14.4 us  [all_to_all(): return lax.all_to_all(x, axes, split_axis=0, concat_axis=0, tiled=True)]
    all_to_all x0 -> x1, blocking collectives: none -> 20.7 us  [all_to_all(): return lax.all_to_all(x, axes, split_axis=0, concat_axis=0, tiled=True)]
    pallas_call x0 -> x3, Pallas kernels: none -> 20.1 us  [the longest x1 11.1 us: per_device(): pl.pallas_call(distance_kernel, out_shape=jax.ShapeDtypeStruct((2, n_mp,...]
    another operation x3 -> x4, other arithmetic: 18.5 us -> 0.04 us  [the longest x2 0.03 us: per_device(): jnp.stack([oth_label, weight])]
    all_to_all x6 -> x3, waiting for transfers between devices: 56.2 us -> 40.7 us  [all_to_all(): return lax.all_to_all(x, axes, split_axis=0, concat_axis=0, tiled=True)]
    dot_general x5 -> x0, matrix products: 12.2 us -> none  [the longest x4 9.56 us: per_device(): picked = jnp.dot(onehot, feature_cents, preferred_element_type=jnp.float32)]
    unnamed x14 -> x6, local copies, waits for them, and re-layouts: 5.58 us -> 0.02 us
  transfers between devices with their start and end apart: 6 -> 5, of which waited for: 3 -> 3; matrix products, arithmetic and copies ran while one was open for 34% -> 5% of each run, Pallas kernels for 0% -> 8%
where the time goes in v1:
time: 104 us
  waiting for transfers between devices  41.7 us (40%)
  blocking collectives  20.7 us (20%)
  Pallas kernels  20.1 us (19%)
  starting transfers between devices  14.8 us (14%)
  local copies, waits for them, and re-layouts  4.93 us (5%)
    all_to_all x3, waiting for transfers between devices, all_to_all(): return lax.all_to_all(x, axes, split_axis=0, concat_axis=0, tiled=True)  40.7 us
    all_to_all x1, blocking collectives, all_to_all(): return lax.all_to_all(x, axes, split_axis=0, concat_axis=0, tiled=True)  20.7 us
    all_to_all x3, starting transfers between devices, all_to_all(): return lax.all_to_all(x, axes, split_axis=0, concat_axis=0, tiled=True)  14.4 us
    pallas_call x1, Pallas kernels, per_device(): pl.pallas_call(distance_kernel, out_shape=jax.ShapeDtypeStruct((2, n_mp,...  11.1 us
    pallas_call x1, Pallas kernels, per_device(): pl.pallas_call(scatter_kernel, out_shape=(jax.ShapeDtypeStruct((half, wid...  8.19 us
    reshape x1, local copies, waits for them, and re-layouts, per_device(): block = centroids.reshape(-1, 2, share, n_mp, width)  3.33 us
  transfers between devices with their start and end apart: 5, of which 3 were waited for; matrix products, arithmetic and copies ran while one was open for 5% of the time, Pallas kernels for 8%

profile of v1, /device:TPU:2, one launch (start us, length us, event | category | flops | bytes accessed | tf_op | source)
XLA Modules:
  0.0 103.7 jit_solution(11190129592012055338)
XLA Ops:
  0.6 0.1 collective-permute-start.1
  0.7 3.3 %reshape.39 = bf16[8,2,64,4,256]{4,3,2,1,0:T(4,128)(2,1)S(1)} reshape(bf16[1024,1024]{1,0:T(8,128)(2,1)} %param.7) | data formatting | bytes 4194304 | tf_op jit(solution)/shard_map/reshape | solution.py:171
  4.1 0.4 constant_dynamic-slice_fusion.1
  4.5 0.0 copy-start.1
  4.5 0.0 copy-start.2
  4.5 0.0 copy-start
  4.5 1.2 %copy.10 = bf16[8,1,64,4,256]{4,2,0,3,1:T(8,128)(2,1)} copy(bf16[8,1,64,4,256]{4,3,2,1,0:T(4,128)(2,1)S(1)} %constant_dynamic-slice_fusion.1) | data formatting | bytes 2097152 | tf_op jit(solution)/shard_map/transpose | solution.py:173
  5.7 5.8 %all-to-all-start = ((bf16[4,512,256]{2,1,0:T(8,128)(2,1)}), bf16[4,512,256]{2,1,0:T(8,128)(2,1)S(1)}, u32[]{:S(2)}, u32[]{:S(2)}) async-start(bf16[4,512,256]{2,1,0:T(8,128)(2,1)} %bitcast.8), calls=%async_computation | async-start | bytes 2097152 | tf_op jit(solution)/shard_map/all_to_all | solution.py:16
  11.4 0.0 copy-done.1
  11.5 0.0 copy-done.2
  11.5 0.3 collective-permute-start
  11.8 1.0 collective-permute-done.oth_aux
  12.8 13.2 %all-to-all-done = bf16[4,512,256]{2,1,0:T(8,128)(2,1)S(1)} async-done(((bf16[4,512,256]{2,1,0:T(8,128)(2,1)}), bf16[4,512,256]{2,1,0:T(8,128)(2,1)S(1)}, u32[]{:S(2)}, u32[]{:S(2)}) %all-to-all-start) | async-done | bytes 1048608 | tf_op jit(solution)/shard_map/all_to_all | solution.py:16
  26.0 0.0 collective-permute-done.1.oth_docs
  26.0 0.0 copy-done
  26.0 11.1 %distances.1 = f32[2,4,24,128]{3,2,1,0:T(8,128)} custom-call(s32[1]{0:T(128)} %bitcast.core, f32[2,16,128]{2,1,0:T(8,128)S(1)} %get-tuple-element.18.own_aux, bf16[2048,256]{1,0:T(8,128)(2,1)S(1)} %copy-done, f32[2,16,128]{2,1,0:T(8,128)S(1)} %collective-permute-done.oth_aux, bf16[2048,256]{1,0:T(8,128)(2,1)} %collective-permute-done.1.oth_docs, ...), custom_call_target="tpu_custom_call" | custom-call | flops 4294967296 | bytes 3145728 | tf_op jit(solution)/shard_map/distances/pallas_call | solution.py:190
  37.1 4.7 %all-to-all-start.1 = ((f32[8,24,128]{2,1,0:T(8,128)}), f32[8,24,128]{2,1,0:T(8,128)S(1)}, u32[]{:S(2)}, u32[]{:S(2)}) async-start(f32[8,24,128]{2,1,0:T(8,128)} %bitcast.10), calls=%async_computation.1 | async-start | bytes 196608 | tf_op jit(solution)/shard_map/all_to_all | solution.py:16
  41.8 8.2 %scatter.1 = (bf16[2048,256]{1,0:T(8,128)(2,1)}, f32[32,128]{1,0:T(8,128)S(1)}) custom-call(f32[2,16,128]{2,1,0:T(8,128)S(1)} %get-tuple-element.18.own_aux, bf16[2048,256]{1,0:T(8,128)(2,1)S(1)} %copy-done, f32[2,16,128]{2,1,0:T(8,128)S(1)} %collective-permute-done.oth_aux, bf16[2048,256]{1,0:T(8,128)(2,1)} %collective-permute-done.1.oth_docs), custom_call_target="tpu_custom_call" | custom-call | flops 4294967296 | bytes 3145728 | tf_op jit(solution)/shard_map/scatter/pallas_call | solution.py:176
  50.0 0.0 all-to-all-done.1
  50.1 20.7 %all_to_all.20.tail = f32[32,8,128]{2,1,0:T(8,128)S(1)} all-to-all(f32[32,8,128]{2,1,0:T(8,128)S(1)} %select_maximum_fusion), channel_id=1, replica_groups=mesh['y'=4,'z'=8,'c'=2,'mp'=4] {'y','z'}, dimensions={0} | all-to-all | bytes 262144 | tf_op jit(solution)/shard_map/all_to_all | solution.py:16
  70.8 3.9 %all-to-all-start.2 = ((bf16[32,64,256]{2,1,0:T(8,128)(2,1)}), bf16[32,64,256]{2,1,0:T(8,128)(2,1)S(1)}, u32[]{:S(2)}, u32[]{:S(2)}) async-start(bf16[32,64,256]{2,1,0:T(8,128)(2,1)} %bitcast.12), calls=%async_computation.2 | async-start | bytes 2097152 | tf_op jit(solution)/shard_map/all_to_all | solution.py:16
  74.7 0.6 fusion.3
  75.3 27.5 %all-to-all-done.2.recv = bf16[32,64,256]{2,1,0:T(8,128)(2,1)S(1)} async-done(((bf16[32,64,256]{2,1,0:T(8,128)(2,1)}), bf16[32,64,256]{2,1,0:T(8,128)(2,1)S(1)}, u32[]{:S(2)}, u32[]{:S(2)}) %all-to-all-start.2) | async-done | bytes 1048608 | tf_op jit(solution)/shard_map/all_to_all | solution.py:16
  102.8 0.8 update.1
  (9 shorter events, 0.1 us)
Async XLA Ops:
  0.6 25.4 %collective-permute-start.1 = (bf16[2048,256]{1,0:T(8,128)(2,1)}, bf16[2048,256]{1,0:T(8,128)(2,1)}, u32[]{:S(2)}, u32[]{:S(2)}) collective-permute-start(bf16[2048,256]{1,0:T(8,128)(2,1)} %own_docs.3), channel_id=1, source_target_pairs={{0,4},{4,0},{1,5},{5,1},{2,6},{6,2},{3,7},{7,3},{8,12},{12,8},{9,1... | collective-permute-start | bytes 3145736 | tf_op jit(solution)/shard_map/ppermute | solution.py:162
  4.5 7.0 %copy-start.1 = (s32[2048]{0:T(1024)S(1)}, s32[2048]{0:T(1024)}, u32[]{:S(2)}) copy-start(s32[2048]{0:T(1024)} %param.5) | copy-start | bytes 24580
  4.5 7.0 %copy-start.2 = (f32[2048]{0:T(1024)S(1)}, f32[2048]{0:T(1024)}, u32[]{:S(2)}) copy-start(f32[2048]{0:T(1024)} %param.6) | copy-start | bytes 24580
  4.5 21.5 %copy-start = (bf16[2048,256]{1,0:T(8,128)(2,1)S(1)}, bf16[2048,256]{1,0:T(8,128)(2,1)}, u32[]{:S(2)}) copy-start(bf16[2048,256]{1,0:T(8,128)(2,1)} %own_docs.3) | copy-start | bytes 3145732
  5.7 20.3 %all-to-all-start = ((bf16[4,512,256]{2,1,0:T(8,128)(2,1)}), bf16[4,512,256]{2,1,0:T(8,128)(2,1)S(1)}, u32[]{:S(2)}, u32[]{:S(2)}) async-start(bf16[4,512,256]{2,1,0:T(8,128)(2,1)} %bitcast.8), calls=%async_computation | async-start | bytes 2097152 | tf_op jit(solution)/shard_map/all_to_all | solution.py:16
  11.5 1.3 %collective-permute-start = (f32[2,16,128]{2,1,0:T(8,128)S(1)}, f32[2,16,128]{2,1,0:T(8,128)S(1)}, u32[]{:S(2)}, u32[]{:S(2)}) collective-permute-start(f32[2,16,128]{2,1,0:T(8,128)S(1)} %get-tuple-element.17), channel_id=1, source_target_pairs={{0,4},{4,0},{1,5},{5,1},{2,6},{6,2},{3,7},{7,3},{8,12},{12,8},{9,1... | collective-permute-start | bytes 49160 | tf_op jit(solution)/shard_map/ppermute | solution.py:169
  37.1 12.9 %all-to-all-start.1 = ((f32[8,24,128]{2,1,0:T(8,128)}), f32[8,24,128]{2,1,0:T(8,128)S(1)}, u32[]{:S(2)}, u32[]{:S(2)}) async-start(f32[8,24,128]{2,1,0:T(8,128)} %bitcast.10), calls=%async_computation.1 | async-start | bytes 196608 | tf_op jit(solution)/shard_map/all_to_all | solution.py:16
  70.8 32.1 %all-to-all-start.2 = ((bf16[32,64,256]{2,1,0:T(8,128)(2,1)}), bf16[32,64,256]{2,1,0:T(8,128)(2,1)S(1)}, u32[]{:S(2)}, u32[]{:S(2)}) async-start(bf16[32,64,256]{2,1,0:T(8,128)(2,1)} %bitcast.12), calls=%async_computation.2 | async-start | bytes 2097152 | tf_op jit(solution)/shard_map/all_to_all | solution.py:16

commit v2 on v0

v2 whole, which is shorter than its diff:
```python
import jax
import jax.numpy as jnp
from jax import lax
from jax.experimental import pallas as pl
from jax.experimental.pallas import tpu as pltpu
from jax.sharding import Mesh, PartitionSpec as P

D = 1024
F32 = jnp.float32
BF16 = jnp.bfloat16
TILE = 256
DOCS = 512
EXTRA = 16
NEAR = (0, 1, 3)
FAR = (2,)
LANES = 128
VMEM = pl.BlockSpec(memory_space=pltpu.VMEM)
SMEM = pl.BlockSpec(memory_space=pltpu.SMEM)
ANY = pl.BlockSpec(memory_space=pl.ANY)


def all_to_all(x, axes):
    return lax.all_to_all(x, axes, split_axis=0, concat_axis=0, tiled=True)


def shifted(x, axis, step):
    size = lax.axis_size(axis)
    return lax.ppermute(x, axis, [(i, (i + step) % size) for i in range(size)])


def cost(flops, moved):
    return pl.CostEstimate(flops=flops, bytes_accessed=moved, transcendentals=0)


def split3(x):
    one = x.astype(BF16)
    rest = x - one.astype(F32)
    two = rest.astype(BF16)
    three = (rest - two.astype(F32)).astype(BF16)
    return one.astype(F32), two.astype(F32), three.astype(F32)


def prep_kernel(assign, quality, cents, own_aux, oth_aux, *outs_and_scratch):
    outs, (label_in, weight_in, block, sems) = outs_and_scratch[:-4], outs_and_scratch[-4:]
    core, me = lax.axis_index("c"), lax.axis_index("mp")
    parts = len(outs)
    share, width = outs[0].shape[1], outs[0].shape[2]
    blocks = block.shape[0]
    copies = [
        pltpu.make_async_copy(cents.at[i, core], block.at[i], sems.at[i]) for i in range(blocks)
    ]
    small = [
        pltpu.make_async_copy(assign, label_in, sems.at[blocks]),
        pltpu.make_async_copy(quality, weight_in, sems.at[blocks + 1]),
    ]
    for copy in small + copies:
        copy.start()
    for copy in small:
        copy.wait()
    label = label_in[...]
    owner = lax.shift_right_logical(label, share.bit_length() - 1)
    local = lax.bitwise_and(label, share - 1)
    half = lax.shift_right_logical(owner, 1) * share + local
    side = lax.bitwise_and(owner, 1)
    weight = weight_in[...].astype(BF16).astype(F32)
    own_aux[0] = jnp.where(side == core, half, -1).astype(F32)
    own_aux[1] = weight
    oth_aux[0] = jnp.where(side == core, -1, half).astype(F32)
    oth_aux[1] = weight
    for i, copy in enumerate(copies):
        copy.wait()
        for s in range(parts):
            to = lax.rem(me + s, parts)
            columns = pl.ds(pl.multiple_of(to * width, width), width)
            outs[s][i] = block[i, :, columns]


def scatter_kernel(own_aux, own_docs, oth_aux, oth_docs, own_sums, *sums):
    rows = own_docs.shape[0]
    quarters = len(sums) + 1
    step = own_sums.shape[0] - EXTRA
    sub = lax.broadcasted_iota(jnp.int32, (TILE, LANES), 0).astype(F32).astype(BF16)
    y = lax.axis_index("y")
    sides = []
    for aux, docs in ((own_aux, own_docs), (oth_aux, oth_docs)):
        label = aux[0].astype(jnp.int32)
        shift = lax.bitwise_and(
            lax.shift_right_arithmetic(label, step.bit_length() - 1) - y, quarters - 1
        )
        moved = jnp.where(label < 0, -1, shift * step + lax.bitwise_and(label, step - 1))
        sides.append((moved.astype(F32), aux[1], docs))

    order = list(range(1, quarters)) + [0]
    for q in order:
        out = own_sums if q == 0 else sums[q - 1]
        for t in range(step // TILE):
            base = float(q * step + t * TILE)
            total = jnp.zeros((TILE, own_docs.shape[1]), F32)
            for label, weight, docs in sides:
                rel = jnp.clip(label - base, -1.0, float(TILE)).astype(BF16)
                weight = weight.astype(BF16)
                hot = jnp.concatenate(
                    [
                        jnp.where(
                            sub == jnp.broadcast_to(rel[r : r + 1], (TILE, LANES)),
                            jnp.broadcast_to(weight[r : r + 1], (TILE, LANES)),
                            jnp.zeros((TILE, LANES), BF16),
                        )
                        for r in range(rows // LANES)
                    ],
                    axis=1,
                )
                total = total + jnp.dot(hot, docs[...], preferred_element_type=F32)
            out[t * TILE : (t + 1) * TILE, :] = total.astype(out.dtype)

    share = own_docs.shape[1] // 4
    owners = quarters * step // share
    owner_sub = lax.broadcasted_iota(jnp.int32, (owners, LANES), 0).astype(F32)
    local_sub = lax.broadcasted_iota(jnp.int32, (share, LANES), 0).astype(F32)
    total = jnp.zeros((owners, 2 * share), F32)
    for label, weight, docs in sides:
        owner = jnp.floor(label * (1.0 / share))
        local = label - owner * share
        owner_hot, local_hot = [], []
        for r in range(rows // LANES):
            owner_hot.append((owner_sub == owner[r : r + 1]).astype(F32))
            same = local_sub == local[r : r + 1]
            local_hot.append(
                jnp.concatenate(
                    [same.astype(F32), jnp.where(same, weight[r : r + 1], 0.0)], axis=0
                )
            )
        total = total + lax.dot_general(
            jnp.concatenate(owner_hot, axis=1).astype(BF16),
            jnp.concatenate(local_hot, axis=1).astype(BF16),
            (((1,), (1,)), ((), ())),
            preferred_element_type=F32,
        )
    packed = jnp.concatenate([total[:, :share], *split3(total[:, share:])], axis=1)
    per = owners // quarters
    for q in order:
        out = own_sums if q == 0 else sums[q - 1]
        piece = packed[q * per : (q + 1) * per]
        pad = jnp.zeros((EXTRA - per, piece.shape[1]), F32)
        out[step:, :] = jnp.concatenate([piece, pad], axis=0).astype(out.dtype)


def squares(label, row_in, docs, tables, shifts):
    step = tables[0].shape[0]
    rows = docs.shape[0]
    per = DOCS // LANES
    parts = lax.axis_size("mp")
    lane = lax.broadcasted_iota(jnp.int32, (DOCS, TILE), 1).astype(F32).astype(BF16)
    shift = lax.bitwise_and(
        lax.axis_index("mp") - lax.shift_right_arithmetic(label, step.bit_length() - 1),
        parts - 1,
    )
    moved = jnp.full(label.shape, -1, jnp.int32)
    for k, s in enumerate(shifts):
        moved = jnp.where(shift == s, k * step + lax.bitwise_and(label, step - 1), moved)
    moved = jnp.where(label < 0, -1, moved).astype(F32)
    result = []
    for i in range(rows // DOCS):
        columns = []
        for j in range(per):
            row = moved[i * per + j : i * per + j + 1]
            columns.append(jnp.broadcast_to(row, (LANES, LANES)).T)
        column = jnp.concatenate(columns, axis=0)
        high = jnp.floor(column * (1.0 / TILE))
        low = (column - high * TILE).astype(BF16)
        high = high.astype(BF16)
        same = jnp.concatenate([low, low], axis=1) == lane
        picked = jnp.zeros((DOCS, docs.shape[1]), F32)
        for k, table in enumerate(tables):
            hots = []
            for t in range(step // TILE):
                hit = jnp.where(
                    high == jnp.full((DOCS, LANES), k * (step // TILE) + t, BF16),
                    jnp.ones((DOCS, LANES), BF16),
                    jnp.zeros((DOCS, LANES), BF16),
                )
                hots.append(
                    jnp.where(
                        same, jnp.concatenate([hit, hit], axis=1), jnp.zeros((DOCS, TILE), BF16)
                    )
                )
            picked = picked + jnp.dot(
                jnp.concatenate(hots, axis=1), table[...], preferred_element_type=F32
            )
        diff = docs[i * DOCS : (i + 1) * DOCS, :].astype(F32) - picked
        square = diff * diff
        folded = square[:, :LANES]
        for k in range(1, square.shape[1] // LANES):
            folded = folded + square[:, k * LANES : (k + 1) * LANES]
        for j in range(per):
            g = i * per + j
            row = jnp.sum(folded[j * LANES : (j + 1) * LANES].T, axis=0, keepdims=True)
            other = 0.0 if row_in is None else row_in[g : g + 1, :]
            result.append(jnp.where(moved[g : g + 1] >= 0.0, row, other))
    return result


def near_kernel(own_aux, own_docs, oth_aux, oth_docs, *rest):
    tables, outs = rest[:-2], rest[-2:]
    for aux, docs, out in ((own_aux, own_docs, outs[0]), (oth_aux, oth_docs, outs[1])):
        label = aux[0].astype(jnp.int32)
        for g, row in enumerate(squares(label, None, docs, tables, NEAR)):
            out[g : g + 1, :] = row


def far_kernel(own_aux, own_docs, oth_aux, oth_docs, own_near, oth_near, *rest):
    tables, (own_out, oth_out, total_out) = rest[:-3], rest[-3:]
    total = jnp.zeros((1, LANES), F32)
    sides = (
        (own_aux, own_docs, own_near, own_out),
        (oth_aux, oth_docs, oth_near, oth_out),
    )
    for aux, docs, near, out in sides:
        label = aux[0].astype(jnp.int32)
        for g, row in enumerate(squares(label, near, docs, tables, FAR)):
            out[g : g + 1, :] = row
            total = total + row
    total_out[...] = jnp.broadcast_to(total[None], total_out.shape)


def combine_kernel(scale, own, *rest):
    arrived, totals, out = rest[:-2], rest[-2], rest[-1]
    step = own.shape[0] - EXTRA
    share, width = out.shape[1] - EXTRA, out.shape[2]
    fold = width // 4
    sums = own[...]
    for other in arrived:
        sums = sums + other[...].astype(F32)
    inertia = jnp.sum(jnp.sum(totals[...], axis=0), axis=1, keepdims=True) * scale
    parts = jnp.concatenate(
        [jnp.broadcast_to(part, (1, fold)) for part in split3(inertia)], axis=1
    )
    for z in range(out.shape[0]):
        out[z, 0:share, :] = sums[z * share : (z + 1) * share].astype(BF16)
        row = sums[step + z : step + z + 1]
        counts = row[:, :fold]
        mass = row[:, fold : 2 * fold] + row[:, 2 * fold : 3 * fold] + row[:, 3 * fold :]
        counts_one, counts_two, _ = split3(counts)
        first = jnp.concatenate([counts_one, *split3(mass)], axis=1)
        second = jnp.concatenate([counts_two, parts], axis=1)
        pad = jnp.zeros((EXTRA - 2, width), F32)
        out[z, share:, :] = jnp.concatenate([first, second, pad], axis=0).astype(BF16)


def update_kernel(recv, old, centroids, quality, inertia):
    share, width = old.shape
    fold = width // 4
    total = recv[0].astype(F32)
    for p in range(1, recv.shape[0]):
        total = total + recv[p].astype(F32)
    first, second = total[share : share + 1], total[share + 1 : share + 2]
    counts = first[:, :fold] + second[:, :fold]
    mass = (first[:, fold : 2 * fold] + first[:, 2 * fold : 3 * fold]) + first[:, 3 * fold :]
    quality[...] = mass / (counts + 1.0)
    inertia[...] = jnp.broadcast_to(
        second[:, fold : fold + 1]
        + second[:, 2 * fold : 2 * fold + 1]
        + second[:, 3 * fold : 3 * fold + 1],
        inertia.shape,
    )
    wide = jnp.concatenate([mass, mass], axis=1)
    wide = jnp.broadcast_to(wide, (LANES, LANES)).T[:share]
    divisor = jnp.concatenate([wide] * (width // LANES), axis=1) + 1.0
    centroids[...] = ((total[:share] + old[...].astype(F32)) / divisor).astype(BF16)


def per_device(documents, assign, quality, centroids):
    rows, width = documents.shape
    y, z = lax.axis_index("y"), lax.axis_index("z")
    me = lax.axis_index("mp")
    n_mp, n_y, n_z = lax.axis_size("mp"), lax.axis_size("y"), lax.axis_size("z")
    clusters = centroids.shape[0] * n_mp
    share = clusters // (2 * n_y * n_z)
    half = clusters // 2
    groups = rows // LANES
    params = pltpu.CompilerParams(vmem_limit_bytes=32 * 1024 * 1024)
    swap = [(0, 1), (1, 0)]

    oth_docs = lax.ppermute(documents, "c", swap)
    blocks = half // n_mp // share
    own_aux, send_aux, *slices = pl.pallas_call(
        prep_kernel,
        out_shape=[jax.ShapeDtypeStruct((2, groups, LANES), F32)] * 2
        + [jax.ShapeDtypeStruct((blocks, share, width), BF16)] * n_mp,
        in_specs=[ANY, ANY, ANY],
        out_specs=[VMEM] * (2 + n_mp),
        scratch_shapes=[
            pltpu.VMEM((groups, LANES), jnp.int32),
            pltpu.VMEM((groups, LANES), F32),
            pltpu.VMEM((blocks, share, n_mp * width), BF16),
            pltpu.SemaphoreType.DMA((blocks + 2,)),
        ],
        cost_estimate=cost(0, 2 * half * width * 2),
        name="prep",
    )(
        assign.reshape(groups, LANES),
        quality.reshape(groups, LANES),
        centroids.reshape(blocks, 2, share, -1),
    )
    oth_aux = lax.ppermute(send_aux, "c", swap)
    slices = [x.reshape(half // n_mp, width) for x in slices]
    tables = [slices[0]] + [shifted(slices[s], "mp", s) for s in range(1, n_mp)]

    quarter = half // n_y
    sums = pl.pallas_call(
        scatter_kernel,
        out_shape=[jax.ShapeDtypeStruct((quarter + EXTRA, width), F32)]
        + [jax.ShapeDtypeStruct((quarter + EXTRA, width), BF16)] * (n_y - 1),
        in_specs=[VMEM] * 4,
        compiler_params=params,
        cost_estimate=cost(4 * rows * half * width, 3 * rows * width * 2),
        name="scatter",
    )(own_aux, documents, oth_aux, oth_docs)
    arrived = [shifted(sums[s], "y", s) for s in range(1, n_y)]

    own_aux, oth_aux, _ = lax.optimization_barrier((own_aux, oth_aux, sums[1]))
    near = pl.pallas_call(
        near_kernel,
        out_shape=[jax.ShapeDtypeStruct((groups, LANES), F32)] * 2,
        in_specs=[VMEM] * (4 + len(NEAR)),
        compiler_params=params,
        cost_estimate=cost(0, 0),
        name="near",
    )(own_aux, documents, oth_aux, oth_docs, *[tables[s] for s in NEAR])
    own_part, oth_part, total = pl.pallas_call(
        far_kernel,
        out_shape=[jax.ShapeDtypeStruct((groups, LANES), F32)] * 2
        + [jax.ShapeDtypeStruct((2 * n_y * n_mp, 1, LANES), F32)],
        in_specs=[VMEM] * (6 + len(FAR)),
        compiler_params=params,
        cost_estimate=cost(0, 0),
        name="far",
    )(own_aux, documents, oth_aux, oth_docs, *near, *[tables[s] for s in FAR])
    totals = all_to_all(total, ("y", "c", "mp"))
    part = own_part + lax.ppermute(oth_part, "c", swap)
    for other in [shifted(part, "mp", s) for s in range(1, n_mp)]:
        part = part + other
    distances = (part / D).reshape(rows)

    total_docs = rows * n_y * n_z * 2
    packed = pl.pallas_call(
        lambda *refs: combine_kernel(1.0 / D / total_docs, *refs),
        out_shape=jax.ShapeDtypeStruct((n_z, share + EXTRA, width), BF16),
        compiler_params=params,
        cost_estimate=cost(0, 6 * quarter * width * 2),
        name="combine",
    )(sums[0], *arrived, totals)
    recv = all_to_all(packed, "z")

    olds = [lax.dynamic_slice_in_dim(x, z * share, share, 0) for x in tables]
    source = lax.rem(me - y + n_mp, n_mp)
    old = olds[0]
    for s in range(1, n_mp):
        old = jnp.where(source == s, olds[s], old)
    new_centroids, cluster_quality, inertia = pl.pallas_call(
        update_kernel,
        out_shape=(
            jax.ShapeDtypeStruct((share, width), BF16),
            jax.ShapeDtypeStruct((1, share), F32),
            jax.ShapeDtypeStruct((1, LANES), F32),
        ),
        compiler_params=params,
        cost_estimate=cost(0, 9 * share * width * 2),
        name="update",
    )(recv, old)
    return distances, new_centroids, cluster_quality.reshape(share), inertia[0, 0]


def solution(mesh):
    n_dp, n_mp = mesh.devices.shape
    n_y, n_z = 4, n_dp // 8
    fine = Mesh(mesh.devices.reshape(n_y, n_z, 2, n_mp), ("y", "z", "c", "mp"))
    dp = ("y", "z", "c")
    return jax.shard_map(
        per_device,
        mesh=fine,
        in_specs=(P(dp, "mp"), P(dp), P(dp), P("mp", None)),
        out_specs=(P(dp), P(dp, "mp"), P(dp), P()),
        check_vma=False,
    )
```

time: 190 us -> 62.2 us (0.33)
  waiting for transfers between devices: 56.2 us -> 8.53 us
  local copies, waits for them, and re-layouts: 48 us -> 0.72 us
  starting transfers between devices: 46.7 us -> 22.6 us
  other arithmetic: 22.4 us -> 0.63 us
  Pallas kernels: 0 us -> 14.6 us
  blocking collectives: 0 us -> 13.8 us
  matrix products: 12.2 us -> 0 us
    all_to_all x6 -> x1, waiting for transfers between devices: 56.2 us -> 4.92 us  [all_to_all(): return lax.all_to_all(x, axes, split_axis=0, concat_axis=0, tiled=True)]
    all_to_all x6 -> x1, starting transfers between devices: 46.7 us -> 8.46 us  [all_to_all(): return lax.all_to_all(x, axes, split_axis=0, concat_axis=0, tiled=True)]
    scatter x3 -> x0, local copies, waits for them, and re-layouts: 33.9 us -> none  [the longest x1 14.6 us: per_device(): jnp.zeros((owners_count * capacity,), jnp.bfloat16).at[slot_index]]
    another operation x3 -> x0, other arithmetic: 18.5 us -> none
    pallas_call x0 -> x6, Pallas kernels: none -> 14.6 us  [the longest x1 4.81 us: per_device(): pl.pallas_call(scatter_kernel, out_shape=[jax.ShapeDtypeStruct((quarter +...]
    ppermute x0 -> x12, starting transfers between devices: none -> 14.2 us  [the longest x9 13.6 us: shifted(): return lax.ppermute(x, axis, [(i, (i + step) % size) for i in range(size)])]
    all_to_all x0 -> x1, blocking collectives: none -> 13.8 us  [all_to_all(): return lax.all_to_all(x, axes, split_axis=0, concat_axis=0, tiled=True)]
    dot_general x5 -> x0, matrix products: 12.2 us -> none  [the longest x4 9.56 us: per_device(): picked = jnp.dot(onehot, feature_cents, preferred_element_type=jnp.float32)]
  transfers between devices with their start and end apart: 6 -> 13, of which waited for: 3 -> 3; matrix products, arithmetic and copies ran while one was open for 34% -> 1% of each run, Pallas kernels for 0% -> 21%
where the time goes in v2:
time: 62.2 us; the launch traced here: 61.7 us
  starting transfers between devices  22.6 us (36%)
  Pallas kernels  14.6 us (23%)
  blocking collectives  13.8 us (22%)
  waiting for transfers between devices  8.53 us (14%)
  between operations  0.73 us (1%)
  local copies, waits for them, and re-layouts  0.72 us (1%)
  other arithmetic  0.63 us (1%)
    all_to_all x1, blocking collectives, all_to_all(): return lax.all_to_all(x, axes, split_axis=0, concat_axis=0, tiled=True)  13.8 us
    ppermute x9, starting transfers between devices, shifted(): return lax.ppermute(x, axis, [(i, (i + step) % size) for i in range(size)])  13.6 us
    all_to_all x1, starting transfers between devices, all_to_all(): return lax.all_to_all(x, axes, split_axis=0, concat_axis=0, tiled=True)  8.46 us
    all_to_all x1, waiting for transfers between devices, all_to_all(): return lax.all_to_all(x, axes, split_axis=0, concat_axis=0, tiled=True)  4.92 us
    pallas_call x1, Pallas kernels, per_device(): pl.pallas_call(scatter_kernel, out_shape=[jax.ShapeDtypeStruct((quarter +...  4.81 us
    pallas_call x1, Pallas kernels, per_device(): pl.pallas_call(near_kernel, out_shape=[jax.ShapeDtypeStruct((groups, LANE...  3.8 us
    ppermute x9, waiting for transfers between devices, shifted(): return lax.ppermute(x, axis, [(i, (i + step) % size) for i in range(size)])  2.46 us
    pallas_call x1, Pallas kernels, per_device(): pl.pallas_call(prep_kernel, out_shape=[jax.ShapeDtypeStruct((2, groups, L...  2.44 us
  transfers between devices with their start and end apart: 13, of which 3 were waited for; matrix products, arithmetic and copies ran while one was open for 1% of the time, Pallas kernels for 21%

profile of v2, /device:TPU:2, one launch (start us, length us, event | category | flops | bytes accessed | tf_op | source)
XLA Modules:
  0.0 61.7 jit_solution(14808909905171453324)
XLA Ops:
  0.6 0.0 copy-start
  0.6 0.1 collective-permute-start.1
  0.7 2.4 %prep.1 = (f32[2,16,128]{2,1,0:T(8,128)}, f32[2,16,128]{2,1,0:T(8,128)}, bf16[8,64,256]{2,1,0:T(8,128)(2,1)}, bf16[8,64,256]{2,1,0:T(8,128)(2,1)}, bf16[8,64,256...) custom-call(s32[16,128]{1,0:T(8,128)} %bitcast.15, f32[16,128]{1,0:T(8,128)} %bitcast.16, bf16[8,2,64,1024]{3,2,1,0:T(8,128)(2,1)} %bitcast.14), custom_call_target="tpu_custom_call" | custom-call | bytes 2097152 | tf_op jit(solution)/shard_map/prep/pallas_call | solution.py:286
  3.2 0.5 collective-permute-start
  3.7 1.5 %collective-permute-start.2 = (bf16[512,256]{1,0:T(8,128)(2,1)}, bf16[512,256]{1,0:T(8,128)(2,1)S(1)}, u32[]{:S(2)}, u32[]{:S(2)}) collective-permute-start(bf16[512,256]{1,0:T(8,128)(2,1)} %bitcast.19), channel_id=1, source_target_pairs={{0,1},{1,2},{2,3},{3,0},{4,5},{5,6},{6,7},{7,4},{8,9},{9,10},{10,1... | collective-permute-start | bytes 786440 | tf_op jit(solution)/shard_map/ppermute | solution.py:28
  5.2 0.8 %collective-permute-start.3 = (bf16[512,256]{1,0:T(8,128)(2,1)}, bf16[512,256]{1,0:T(8,128)(2,1)S(1)}, u32[]{:S(2)}, u32[]{:S(2)}) collective-permute-start(bf16[512,256]{1,0:T(8,128)(2,1)} %bitcast.18), channel_id=1, source_target_pairs={{0,3},{1,0},{2,1},{3,2},{4,7},{5,4},{6,5},{7,6},{8,11},{9,8},{10,9... | collective-permute-start | bytes 786440 | tf_op jit(solution)/shard_map/ppermute | solution.py:28
  6.0 2.1 %collective-permute-start.4 = (bf16[512,256]{1,0:T(8,128)(2,1)}, bf16[512,256]{1,0:T(8,128)(2,1)S(1)}, u32[]{:S(2)}, u32[]{:S(2)}) collective-permute-start(bf16[512,256]{1,0:T(8,128)(2,1)} %bitcast.17), channel_id=1, source_target_pairs={{0,2},{1,3},{2,0},{3,1},{4,6},{5,7},{6,4},{7,5},{8,10},{9,11},{10,... | collective-permute-start | bytes 786440 | tf_op jit(solution)/shard_map/ppermute | solution.py:28
  8.0 0.0 collective-permute-done.oth_aux
  8.0 0.0 collective-permute-done.1.oth_docs
  8.0 0.0 copy-done
  8.1 0.0 copy-start.2
  8.1 0.7 %copy-done.2 = f32[2,16,128]{2,1,0:T(8,128)S(1)} copy-done((f32[2,16,128]{2,1,0:T(8,128)S(1)}, f32[2,16,128]{2,1,0:T(8,128)}, u32[]{:S(2)}) %copy-start.2) | copy-done | bytes 16408
  8.8 0.0 copy-start.1
  8.8 4.8 %scatter.1 = (f32[528,256]{1,0:T(8,128)S(1)}, bf16[528,256]{1,0:T(8,128)(2,1)S(1)}, bf16[528,256]{1,0:T(8,128)(2,1)S(1)}, bf16[528,256]{1,0:T(8,128)(2,1)S(1)}) custom-call(f32[2,16,128]{2,1,0:T(8,128)S(1)} %copy-done.2, bf16[2048,256]{1,0:T(8,128)(2,1)S(1)} %copy-done, f32[2,16,128]{2,1,0:T(8,128)S(1)} %collective-permute-done.oth_aux, ...), custom_call_target="tpu_custom_call" | custom-call | flops 4294967296 | bytes 3145728 | tf_op jit(solution)/shard_map/scatter/pallas_call | solution.py:310
  13.6 3.1 %collective-permute-start.10 = (bf16[528,256]{1,0:T(8,128)(2,1)S(1)}, bf16[528,256]{1,0:T(8,128)(2,1)S(1)}, u32[]{:S(2)}, u32[]{:S(2)}) collective-permute-start(bf16[528,256]{1,0:T(8,128)(2,1)S(1)} %get-tuple-element.38), channel_id=1, source_target_pairs={{0,128},{64,192},{128,0},{192,64},{1,129},{65,193},{129,1},{193,65... | collective-permute-start | bytes 811016 | tf_op jit(solution)/shard_map/ppermute | solution.py:28
  16.6 1.1 %collective-permute-start.11 = (bf16[528,256]{1,0:T(8,128)(2,1)S(1)}, bf16[528,256]{1,0:T(8,128)(2,1)S(1)}, u32[]{:S(2)}, u32[]{:S(2)}) collective-permute-start(bf16[528,256]{1,0:T(8,128)(2,1)S(1)} %get-tuple-element.39), channel_id=1, source_target_pairs={{0,192},{64,0},{128,64},{192,128},{1,193},{65,1},{129,65},{193,129... | collective-permute-start | bytes 811016 | tf_op jit(solution)/shard_map/ppermute | solution.py:28
  17.7 0.0 collective-permute-done.2.rest_1_
  17.7 1.0 %collective-permute-start.9 = (bf16[528,256]{1,0:T(8,128)(2,1)S(1)}, bf16[528,256]{1,0:T(8,128)(2,1)S(1)}, u32[]{:S(2)}, u32[]{:S(2)}) collective-permute-start(bf16[528,256]{1,0:T(8,128)(2,1)S(1)} %get-tuple-element.26), channel_id=1, source_target_pairs={{0,64},{64,128},{128,192},{192,0},{1,65},{65,129},{129,193},{193,1... | collective-permute-start | bytes 811016 | tf_op jit(solution)/shard_map/ppermute | solution.py:28
  18.7 0.0 collective-permute-done.3.rest_2_
  18.7 0.0 copy-done.1
  18.7 3.8 %near.1 = (f32[16,128]{1,0:T(8,128)S(1)}, f32[16,128]{1,0:T(8,128)S(1)}) custom-call(f32[2,16,128]{2,1,0:T(8,128)S(1)} %copy-done.2, bf16[2048,256]{1,0:T(8,128)(2,1)S(1)} %copy-done, f32[2,16,128]{2,1,0:T(8,128)S(1)} %collective-permute-done.oth_aux, bf16[2048,256]{1,0:T(8,128)(2,1)S(1)} %collective-permute-done.1.oth_docs, bf16[512,256]{1,0:T(8,128)(2,1)S(1)} %bitcast.12, ...), custom_call_target="tpu_custom_call" | custom-call | tf_op jit(solution)/shard_map/near/pallas_call | solution.py:322
  22.5 0.0 collective-permute-done.4.rest_0_
  22.5 1.6 %far.1 = (f32[16,128]{1,0:T(8,128)S(1)}, f32[16,128]{1,0:T(8,128)S(1)}, f32[32,1,128]{2,1,0:T(1,128)S(1)}) custom-call(f32[2,16,128]{2,1,0:T(8,128)S(1)} %copy-done.2, bf16[2048,256]{1,0:T(8,128)(2,1)S(1)} %copy-done, f32[2,16,128]{2,1,0:T(8,128)S(1)} %collective-permute-done.oth_aux, bf16[2048,256]{1,0:T(8,128)(2,1)S(1)} %collective-permute-done.1.oth_docs, ...), custom_call_target="tpu_custom_call" | custom-call | tf_op jit(solution)/shard_map/far/pallas_call | solution.py:330
  24.1 13.8 %all_to_all.10.refs_4_ = f32[32,1,128]{2,1,0:T(1,128)S(1)} all-to-all(f32[32,1,128]{2,1,0:T(1,128)S(1)} %get-tuple-element.40), channel_id=1, replica_groups=mesh['y'=4,'z'=8,'c'=2,'mp'=4] {'y','c','mp'}, dimensions={0} | all-to-all | bytes 32768 | tf_op jit(solution)/shard_map/all_to_all | solution.py:23
  38.0 0.0 collective-permute-done.10.refs_2_
  38.0 0.0 collective-permute-done.11.refs_3_
  38.0 0.0 collective-permute-done.9.refs_1_
  38.0 1.1 %combine.1 = bf16[8,80,256]{2,1,0:T(8,128)(2,1)} custom-call(f32[528,256]{1,0:T(8,128)S(1)} %get-tuple-element.37.refs_0_, bf16[528,256]{1,0:T(8,128)(2,1)S(1)} %collective-permute-done.9.refs_1_, bf16[528,256]{1,0:T(8,128)(2,1)S(1)} %collective-permute-done.10.refs_2_, bf16[528,256]{1,0:T(8,128)(2,1)S(1)} %collective-permute-done.11.refs_3_, ...), custom_call_target="tpu_custom_call" | custom-call | bytes 1572864 | tf_op jit(solution)/shard_map/combine/pallas_call | solution.py:346
  39.1 8.5 %all-to-all-start.1 = ((bf16[8,80,256]{2,1,0:T(8,128)(2,1)}), bf16[8,80,256]{2,1,0:T(8,128)(2,1)S(1)}, u32[]{:S(2)}, u32[]{:S(2)}) async-start(bf16[8,80,256]{2,1,0:T(8,128)(2,1)} %combine.1), calls=%async_computation.1 | async-start | bytes 655360 | tf_op jit(solution)/shard_map/all_to_all | solution.py:23
  47.5 0.0 collective-permute-start.5
  47.6 1.1 %collective-permute-done.5 = f32[16,128]{1,0:T(8,128)S(1)} collective-permute-done((f32[16,128]{1,0:T(8,128)S(1)}, f32[16,128]{1,0:T(8,128)S(1)}, u32[]{:S(2)}, u32[]{:S(2)}) %collective-permute-start.5) | collective-permute-done | bytes 8224 | tf_op jit(solution)/shard_map/ppermute | solution.py:340
  48.7 1.5 %collective-permute-start.8 = (f32[16,128]{1,0:T(8,128)S(1)}, f32[16,128]{1,0:T(8,128)S(1)}, u32[]{:S(2)}, u32[]{:S(2)}) collective-permute-start(f32[16,128]{1,0:T(8,128)S(1)} %add.21), channel_id=1, source_target_pairs={{0,3},{1,0},{2,1},{3,2},{4,7},{5,4},{6,5},{7,6},{8,11},{9,8},{10,9... | collective-permute-start | bytes 24584 | tf_op jit(solution)/shard_map/ppermute | solution.py:28
  50.2 0.6 collective-permute-start.7
  50.8 2.1 %collective-permute-start.6 = (f32[16,128]{1,0:T(8,128)S(1)}, f32[16,128]{1,0:T(8,128)S(1)}, u32[]{:S(2)}, u32[]{:S(2)}) collective-permute-start(f32[16,128]{1,0:T(8,128)S(1)} %add.21), channel_id=1, source_target_pairs={{0,1},{1,2},{2,3},{3,0},{4,5},{5,6},{6,7},{7,4},{8,9},{9,10},{10,1... | collective-permute-start | bytes 24584 | tf_op jit(solution)/shard_map/ppermute | solution.py:28
  52.9 0.0 collective-permute-done.8
  52.9 2.4 %collective-permute-done.7 = f32[16,128]{1,0:T(8,128)S(1)} collective-permute-done((f32[16,128]{1,0:T(8,128)S(1)}, f32[16,128]{1,0:T(8,128)S(1)}, u32[]{:S(2)}, u32[]{:S(2)}) %collective-permute-start.7) | collective-permute-done | bytes 8224 | tf_op jit(solution)/shard_map/ppermute | solution.py:28
  55.3 0.0 collective-permute-done.6
  55.3 0.6 multiply_bitcast_fusion
  55.9 4.9 %all-to-all-done.1.recv = bf16[8,80,256]{2,1,0:T(8,128)(2,1)S(1)} async-done(((bf16[8,80,256]{2,1,0:T(8,128)(2,1)}), bf16[8,80,256]{2,1,0:T(8,128)(2,1)S(1)}, u32[]{:S(2)}, u32[]{:S(2)}) %all-to-all-start.1) | async-done | bytes 327712 | tf_op jit(solution)/shard_map/all_to_all | solution.py:23
  60.9 0.9 %update.1 = (bf16[64,256]{1,0:T(8,128)(2,1)}, f32[1,64]{1,0:T(1,128)}, f32[1,128]{1,0:T(1,128)}) custom-call(bf16[8,80,256]{2,1,0:T(8,128)(2,1)S(1)} %all-to-all-done.1.recv, bf16[64,256]{1,0:T(8,128)(2,1)S(1)} %select_select_fusion.old), custom_call_target="tpu_custom_call" | custom-call | bytes 294912 | tf_op jit(solution)/shard_map/update/pallas_call | solution.py:360
  (2 shorter events, 0.0 us)
Async XLA Ops:
  0.6 7.4 %copy-start = (bf16[2048,256]{1,0:T(8,128)(2,1)S(1)}, bf16[2048,256]{1,0:T(8,128)(2,1)}, u32[]{:S(2)}) copy-start(bf16[2048,256]{1,0:T(8,128)(2,1)} %own_docs.5) | copy-start | bytes 3145732
  0.6 7.4 %collective-permute-start.1 = (bf16[2048,256]{1,0:T(8,128)(2,1)}, bf16[2048,256]{1,0:T(8,128)(2,1)S(1)}, u32[]{:S(2)}, u32[]{:S(2)}) collective-permute-start(bf16[2048,256]{1,0:T(8,128)(2,1)} %own_docs.5), channel_id=1, source_target_pairs={{0,4},{4,0},{1,5},{5,1},{2,6},{6,2},{3,7},{7,3},{8,12},{12,8},{9,1... | collective-permute-start | bytes 3145736 | tf_op jit(solution)/shard_map/ppermute | solution.py:284
  3.2 4.9 %collective-permute-start = (f32[2,16,128]{2,1,0:T(8,128)}, f32[2,16,128]{2,1,0:T(8,128)S(1)}, u32[]{:S(2)}, u32[]{:S(2)}) collective-permute-start(f32[2,16,128]{2,1,0:T(8,128)} %get-tuple-element.25), channel_id=1, source_target_pairs={{0,4},{4,0},{1,5},{5,1},{2,6},{6,2},{3,7},{7,3},{8,12},{12,8},{9,1... | collective-permute-start | bytes 49160 | tf_op jit(solution)/shard_map/ppermute | solution.py:305
  3.7 14.0 %collective-permute-start.2 = (bf16[512,256]{1,0:T(8,128)(2,1)}, bf16[512,256]{1,0:T(8,128)(2,1)S(1)}, u32[]{:S(2)}, u32[]{:S(2)}) collective-permute-start(bf16[512,256]{1,0:T(8,128)(2,1)} %bitcast.19), channel_id=1, source_target_pairs={{0,1},{1,2},{2,3},{3,0},{4,5},{5,6},{6,7},{7,4},{8,9},{9,10},{10,1... | collective-permute-start | bytes 786440 | tf_op jit(solution)/shard_map/ppermute | solution.py:28
  5.2 13.5 %collective-permute-start.3 = (bf16[512,256]{1,0:T(8,128)(2,1)}, bf16[512,256]{1,0:T(8,128)(2,1)S(1)}, u32[]{:S(2)}, u32[]{:S(2)}) collective-permute-start(bf16[512,256]{1,0:T(8,128)(2,1)} %bitcast.18), channel_id=1, source_target_pairs={{0,3},{1,0},{2,1},{3,2},{4,7},{5,4},{6,5},{7,6},{8,11},{9,8},{10,9... | collective-permute-start | bytes 786440 | tf_op jit(solution)/shard_map/ppermute | solution.py:28
  6.0 16.5 %collective-permute-start.4 = (bf16[512,256]{1,0:T(8,128)(2,1)}, bf16[512,256]{1,0:T(8,128)(2,1)S(1)}, u32[]{:S(2)}, u32[]{:S(2)}) collective-permute-start(bf16[512,256]{1,0:T(8,128)(2,1)} %bitcast.17), channel_id=1, source_target_pairs={{0,2},{1,3},{2,0},{3,1},{4,6},{5,7},{6,4},{7,5},{8,10},{9,11},{10,... | collective-permute-start | bytes 786440 | tf_op jit(solution)/shard_map/ppermute | solution.py:28
  8.1 0.7 %copy-start.2 = (f32[2,16,128]{2,1,0:T(8,128)S(1)}, f32[2,16,128]{2,1,0:T(8,128)}, u32[]{:S(2)}) copy-start(f32[2,16,128]{2,1,0:T(8,128)} %get-tuple-element.27.own_aux) | copy-start | bytes 49156
  8.8 9.9 %copy-start.1 = (bf16[8,64,256]{2,1,0:T(8,128)(2,1)S(1)}, bf16[8,64,256]{2,1,0:T(8,128)(2,1)}, u32[]{:S(2)}) copy-start(bf16[8,64,256]{2,1,0:T(8,128)(2,1)} %get-tuple-element.29) | copy-start | bytes 786436
  13.6 24.4 %collective-permute-start.10 = (bf16[528,256]{1,0:T(8,128)(2,1)S(1)}, bf16[528,256]{1,0:T(8,128)(2,1)S(1)}, u32[]{:S(2)}, u32[]{:S(2)}) collective-permute-start(bf16[528,256]{1,0:T(8,128)(2,1)S(1)} %get-tuple-element.38), channel_id=1, source_target_pairs={{0,128},{64,192},{128,0},{192,64},{1,129},{65,193},{129,1},{193,65... | collective-permute-start | bytes 811016 | tf_op jit(solution)/shard_map/ppermute | solution.py:28
  16.6 21.3 %collective-permute-start.11 = (bf16[528,256]{1,0:T(8,128)(2,1)S(1)}, bf16[528,256]{1,0:T(8,128)(2,1)S(1)}, u32[]{:S(2)}, u32[]{:S(2)}) collective-permute-start(bf16[528,256]{1,0:T(8,128)(2,1)S(1)} %get-tuple-element.39), channel_id=1, source_target_pairs={{0,192},{64,0},{128,64},{192,128},{1,193},{65,1},{129,65},{193,129... | collective-permute-start | bytes 811016 | tf_op jit(solution)/shard_map/ppermute | solution.py:28
  17.7 20.3 %collective-permute-start.9 = (bf16[528,256]{1,0:T(8,128)(2,1)S(1)}, bf16[528,256]{1,0:T(8,128)(2,1)S(1)}, u32[]{:S(2)}, u32[]{:S(2)}) collective-permute-start(bf16[528,256]{1,0:T(8,128)(2,1)S(1)} %get-tuple-element.26), channel_id=1, source_target_pairs={{0,64},{64,128},{128,192},{192,0},{1,65},{65,129},{129,193},{193,1... | collective-permute-start | bytes 811016 | tf_op jit(solution)/shard_map/ppermute | solution.py:28
  39.1 21.8 %all-to-all-start.1 = ((bf16[8,80,256]{2,1,0:T(8,128)(2,1)}), bf16[8,80,256]{2,1,0:T(8,128)(2,1)S(1)}, u32[]{:S(2)}, u32[]{:S(2)}) async-start(bf16[8,80,256]{2,1,0:T(8,128)(2,1)} %combine.1), calls=%async_computation.1 | async-start | bytes 655360 | tf_op jit(solution)/shard_map/all_to_all | solution.py:23
  47.5 1.2 %collective-permute-start.5 = (f32[16,128]{1,0:T(8,128)S(1)}, f32[16,128]{1,0:T(8,128)S(1)}, u32[]{:S(2)}, u32[]{:S(2)}) collective-permute-start(f32[16,128]{1,0:T(8,128)S(1)} %get-tuple-element.36), channel_id=1, source_target_pairs={{0,4},{4,0},{1,5},{5,1},{2,6},{6,2},{3,7},{7,3},{8,12},{12,8},{9,1... | collective-permute-start | bytes 24584 | tf_op jit(solution)/shard_map/ppermute | solution.py:340
  48.7 4.2 %collective-permute-start.8 = (f32[16,128]{1,0:T(8,128)S(1)}, f32[16,128]{1,0:T(8,128)S(1)}, u32[]{:S(2)}, u32[]{:S(2)}) collective-permute-start(f32[16,128]{1,0:T(8,128)S(1)} %add.21), channel_id=1, source_target_pairs={{0,3},{1,0},{2,1},{3,2},{4,7},{5,4},{6,5},{7,6},{8,11},{9,8},{10,9... | collective-permute-start | bytes 24584 | tf_op jit(solution)/shard_map/ppermute | solution.py:28
  50.2 5.2 %collective-permute-start.7 = (f32[16,128]{1,0:T(8,128)S(1)}, f32[16,128]{1,0:T(8,128)S(1)}, u32[]{:S(2)}, u32[]{:S(2)}) collective-permute-start(f32[16,128]{1,0:T(8,128)S(1)} %add.21), channel_id=1, source_target_pairs={{0,2},{1,3},{2,0},{3,1},{4,6},{5,7},{6,4},{7,5},{8,10},{9,11},{10,... | collective-permute-start | bytes 24584 | tf_op jit(solution)/shard_map/ppermute | solution.py:28
  50.8 4.6 %collective-permute-start.6 = (f32[16,128]{1,0:T(8,128)S(1)}, f32[16,128]{1,0:T(8,128)S(1)}, u32[]{:S(2)}, u32[]{:S(2)}) collective-permute-start(f32[16,128]{1,0:T(8,128)S(1)} %add.21), channel_id=1, source_target_pairs={{0,1},{1,2},{2,3},{3,0},{4,5},{5,6},{6,7},{7,4},{8,9},{9,10},{10,1... | collective-permute-start | bytes 24584 | tf_op jit(solution)/shard_map/ppermute | solution.py:28

commit v3 on v2

--- a/solution.py
+++ b/solution.py
@@ -40,7 +40,18 @@
     return one.astype(F32), two.astype(F32), three.astype(F32)
 
 
-def prep_kernel(assign, quality, cents, own_aux, oth_aux, *outs_and_scratch):
+def placed(label, share):
+    owner = lax.shift_right_logical(label, share.bit_length() - 1)
+    local = lax.bitwise_and(label, share - 1)
+    return lax.bitwise_and(owner, 1), lax.shift_right_logical(owner, 1) * share + local
+
+
+def own_labels(assign, share):
+    side, half = placed(assign[...], share)
+    return jnp.where(side == lax.axis_index("c"), half, -1)
+
+
+def prep_kernel(assign, quality, cents, oth_aux, *outs_and_scratch):
     outs, (label_in, weight_in, block, sems) = outs_and_scratch[:-4], outs_and_scratch[-4:]
     core, me = lax.axis_index("c"), lax.axis_index("mp")
     parts = len(outs)
@@ -57,16 +68,9 @@
         copy.start()
     for copy in small:
         copy.wait()
-    label = label_in[...]
-    owner = lax.shift_right_logical(label, share.bit_length() - 1)
-    local = lax.bitwise_and(label, share - 1)
-    half = lax.shift_right_logical(owner, 1) * share + local
-    side = lax.bitwise_and(owner, 1)
-    weight = weight_in[...].astype(BF16).astype(F32)
-    own_aux[0] = jnp.where(side == core, half, -1).astype(F32)
-    own_aux[1] = weight
+    side, half = placed(label_in[...], share)
     oth_aux[0] = jnp.where(side == core, -1, half).astype(F32)
-    oth_aux[1] = weight
+    oth_aux[1] = weight_in[...].astype(BF16).astype(F32)
     for i, copy in enumerate(copies):
         copy.wait()
         for s in range(parts):
@@ -75,20 +79,24 @@
             outs[s][i] = block[i, :, columns]
 
 
-def scatter_kernel(own_aux, own_docs, oth_aux, oth_docs, own_sums, *sums):
+def scatter_kernel(assign, quality, own_docs, oth_aux, oth_docs, own_sums, *sums):
     rows = own_docs.shape[0]
     quarters = len(sums) + 1
     step = own_sums.shape[0] - EXTRA
     sub = lax.broadcasted_iota(jnp.int32, (TILE, LANES), 0).astype(F32).astype(BF16)
     y = lax.axis_index("y")
     sides = []
-    for aux, docs in ((own_aux, own_docs), (oth_aux, oth_docs)):
-        label = aux[0].astype(jnp.int32)
+    share = own_docs.shape[1] // 4
+    own_weight = quality[...].astype(BF16).astype(F32)
+    for label, weight, docs in (
+        (own_labels(assign, share), own_weight, own_docs),
+        (oth_aux[0].astype(jnp.int32), oth_aux[1], oth_docs),
+    ):
         shift = lax.bitwise_and(
             lax.shift_right_arithmetic(label, step.bit_length() - 1) - y, quarters - 1
         )
         moved = jnp.where(label < 0, -1, shift * step + lax.bitwise_and(label, step - 1))
-        sides.append((moved.astype(F32), aux[1], docs))
+        sides.append((moved.astype(F32), weight, docs))
 
     order = list(range(1, quarters)) + [0]
     for q in order:
@@ -113,7 +121,6 @@
                 total = total + jnp.dot(hot, docs[...], preferred_element_type=F32)
             out[t * TILE : (t + 1) * TILE, :] = total.astype(out.dtype)
 
-    share = own_docs.shape[1] // 4
     owners = quarters * step // share
     owner_sub = lax.broadcasted_iota(jnp.int32, (owners, LANES), 0).astype(F32)
     local_sub = lax.broadcasted_iota(jnp.int32, (share, LANES), 0).astype(F32)
@@ -200,23 +207,36 @@
     return result
 
 
-def near_kernel(own_aux, own_docs, oth_aux, oth_docs, *rest):
-    tables, outs = rest[:-2], rest[-2:]
-    for aux, docs, out in ((own_aux, own_docs, outs[0]), (oth_aux, oth_docs, outs[1])):
-        label = aux[0].astype(jnp.int32)
+def keep_old(out, before, tables, shifts):
+    share, parts = out.shape[0], lax.axis_size("mp")
+    source = lax.rem(lax.axis_index("mp") - lax.axis_index("y") + parts, parts)
+    first = pl.multiple_of(lax.axis_index("z") * share, share)
+    out[...] = jnp.zeros(out.shape, out.dtype) if before is None else before[...]
+    for s, table in zip(shifts, tables):
+
+        @pl.when(source == s)
+        def _():
+            out[...] = table[pl.ds(first, share), :]
+
+
+def near_kernel(assign, own_docs, oth_aux, oth_docs, *rest):
+    tables, outs, old = rest[:-3], rest[-3:-1], rest[-1]
+    keep_old(old, None, tables, NEAR)
+    own, oth = own_labels(assign, own_docs.shape[1] // 4), oth_aux[0].astype(jnp.int32)
+    for label, docs, out in ((own, own_docs, outs[0]), (oth, oth_docs, outs[1])):
         for g, row in enumerate(squares(label, None, docs, tables, NEAR)):
             out[g : g + 1, :] = row
 
 
-def far_kernel(own_aux, own_docs, oth_aux, oth_docs, own_near, oth_near, *rest):
-    tables, (own_out, oth_out, total_out) = rest[:-3], rest[-3:]
+def far_kernel(assign, own_docs, oth_aux, oth_docs, own_near, oth_near, before, *rest):
+    tables, (own_out, oth_out, total_out, old) = rest[:-4], rest[-4:]
+    keep_old(old, before, tables, FAR)
     total = jnp.zeros((1, LANES), F32)
     sides = (
-        (own_aux, own_docs, own_near, own_out),
-        (oth_aux, oth_docs, oth_near, oth_out),
-    )
-    for aux, docs, near, out in sides:
-        label = aux[0].astype(jnp.int32)
+        (own_labels(assign, own_docs.shape[1] // 4), own_docs, own_near, own_out),
+        (oth_aux[0].astype(jnp.int32), oth_docs, oth_near, oth_out),
+    )
+    for label, docs, near, out in sides:
         for g, row in enumerate(squares(label, near, docs, tables, FAR)):
             out[g : g + 1, :] = row
             total = total + row
@@ -271,8 +291,6 @@
 
 def per_device(documents, assign, quality, centroids):
     rows, width = documents.shape
-    y, z = lax.axis_index("y"), lax.axis_index("z")
-    me = lax.axis_index("mp")
     n_mp, n_y, n_z = lax.axis_size("mp"), lax.axis_size("y"), lax.axis_size("z")
     clusters = centroids.shape[0] * n_mp
     share = clusters // (2 * n_y * n_z)
@@ -283,12 +301,14 @@
 
     oth_docs = lax.ppermute(documents, "c", swap)
     blocks = half // n_mp // share
-    own_aux, send_aux, *slices = pl.pallas_call(
+    assign = assign.reshape(groups, LANES)
+    quality = quality.reshape(groups, LANES)
+    send_aux, *slices = pl.pallas_call(
         prep_kernel,
-        out_shape=[jax.ShapeDtypeStruct((2, groups, LANES), F32)] * 2
+        out_shape=[jax.ShapeDtypeStruct((2, groups, LANES), F32)]
         + [jax.ShapeDtypeStruct((blocks, share, width), BF16)] * n_mp,
         in_specs=[ANY, ANY, ANY],
-        out_specs=[VMEM] * (2 + n_mp),
+        out_specs=[VMEM] * (1 + n_mp),
         scratch_shapes=[
             pltpu.VMEM((groups, LANES), jnp.int32),
             pltpu.VMEM((groups, LANES), F32),
@@ -298,44 +318,50 @@
         cost_estimate=cost(0, 2 * half * width * 2),
         name="prep",
     )(
-        assign.reshape(groups, LANES),
-        quality.reshape(groups, LANES),
+        assign,
+        quality,
         centroids.reshape(blocks, 2, share, -1),
     )
     oth_aux = lax.ppermute(send_aux, "c", swap)
     slices = [x.reshape(half // n_mp, width) for x in slices]
-    tables = [slices[0]] + [shifted(slices[s], "mp", s) for s in range(1, n_mp)]
 
     quarter = half // n_y
     sums = pl.pallas_call(
         scatter_kernel,
         out_shape=[jax.ShapeDtypeStruct((quarter + EXTRA, width), F32)]
         + [jax.ShapeDtypeStruct((quarter + EXTRA, width), BF16)] * (n_y - 1),
-        in_specs=[VMEM] * 4,
+        in_specs=[VMEM] * 5,
         compiler_params=params,
         cost_estimate=cost(4 * rows * half * width, 3 * rows * width * 2),
         name="scatter",
-    )(own_aux, documents, oth_aux, oth_docs)
-    arrived = [shifted(sums[s], "y", s) for s in range(1, n_y)]
-
-    own_aux, oth_aux, _ = lax.optimization_barrier((own_aux, oth_aux, sums[1]))
+    )(assign, quality, documents, oth_aux, oth_docs)
+    slices[2], _ = lax.optimization_barrier((slices[2], sums[1]))
+    tables = [slices[0]] + [shifted(slices[s], "mp", s) for s in range(1, n_mp)]
+
+    oth_aux, _ = lax.optimization_barrier((oth_aux, sums[1]))
     near = pl.pallas_call(
         near_kernel,
-        out_shape=[jax.ShapeDtypeStruct((groups, LANES), F32)] * 2,
+        out_shape=[jax.ShapeDtypeStruct((groups, LANES), F32)] * 2
+        + [jax.ShapeDtypeStruct((share, width), BF16)],
         in_specs=[VMEM] * (4 + len(NEAR)),
         compiler_params=params,
         cost_estimate=cost(0, 0),
         name="near",
-    )(own_aux, documents, oth_aux, oth_docs, *[tables[s] for s in NEAR])
-    own_part, oth_part, total = pl.pallas_call(
+    )(assign, documents, oth_aux, oth_docs, *[tables[s] for s in NEAR])
+    *moving, near = lax.optimization_barrier((*sums[1:], near))
+    arrived = [shifted(x, "y", s + 1) for s, x in enumerate(moving)]
+    own_part, oth_part, total, old = pl.pallas_call(
         far_kernel,
         out_shape=[jax.ShapeDtypeStruct((groups, LANES), F32)] * 2
-        + [jax.ShapeDtypeStruct((2 * n_y * n_mp, 1, LANES), F32)],
-        in_specs=[VMEM] * (6 + len(FAR)),
+        + [
+            jax.ShapeDtypeStruct((2 * n_y * n_mp, 1, LANES), F32),
+            jax.ShapeDtypeStruct((share, width), BF16),
+        ],
+        in_specs=[VMEM] * (7 + len(FAR)),
         compiler_params=params,
         cost_estimate=cost(0, 0),
         name="far",
-    )(own_aux, documents, oth_aux, oth_docs, *near, *[tables[s] for s in FAR])
+    )(assign, documents, oth_aux, oth_docs, *near, *[tables[s] for s in FAR])
     totals = all_to_all(total, ("y", "c", "mp"))
     part = own_part + lax.ppermute(oth_part, "c", swap)
     for other in [shifted(part, "mp", s) for s in range(1, n_mp)]:
@@ -352,11 +378,6 @@
     )(sums[0], *arrived, totals)
     recv = all_to_all(packed, "z")
 
-    olds = [lax.dynamic_slice_in_dim(x, z * share, share, 0) for x in tables]
-    source = lax.rem(me - y + n_mp, n_mp)
-    old = olds[0]
-    for s in range(1, n_mp):
-        old = jnp.where(source == s, olds[s], old)
     new_centroids, cluster_quality, inertia = pl.pallas_call(
         update_kernel,
         out_shape=(

time: 62.2 us -> 61 us (0.981)
  blocking collectives: 13.8 us -> 0 us
  waiting for transfers between devices: 8.53 us -> 14.6 us
  starting transfers between devices: 22.6 us -> 28.3 us
  Pallas kernels: 14.6 us -> 16.3 us
  local copies, waits for them, and re-layouts: 0.72 us -> 0.02 us
    all_to_all x1 -> x0, blocking collectives: 13.8 us -> none  [all_to_all(): return lax.all_to_all(x, axes, split_axis=0, concat_axis=0, tiled=True)]
    all_to_all x1 -> x2, starting transfers between devices: 8.46 us -> 13.5 us  [all_to_all(): return lax.all_to_all(x, axes, split_axis=0, concat_axis=0, tiled=True)]
    all_to_all x1 -> x2, waiting for transfers between devices: 4.92 us -> 9.2 us  [all_to_all(): return lax.all_to_all(x, axes, split_axis=0, concat_axis=0, tiled=True)]
    ppermute x9, waiting for transfers between devices: 2.46 us -> 4.24 us  [shifted(): return lax.ppermute(x, axis, [(i, (i + step) % size) for i in range(size)])]
    pallas_call x1, Pallas kernels: 4.81 us -> 5.72 us  [per_device(): pl.pallas_call(scatter_kernel, out_shape=[jax.ShapeDtypeStruct((quarter +...]
    unnamed x6 -> x10, local copies, waits for them, and re-layouts: 0.72 us -> 0.02 us
    pallas_call x1, Pallas kernels: 1.64 us -> 2.29 us  [per_device(): pl.pallas_call(far_kernel, out_shape=[jax.ShapeDtypeStruct((groups, LANES...]
  transfers between devices with their start and end apart: 13 -> 14, of which waited for: 3 -> 5; matrix products, arithmetic and copies ran while one was open for 1% -> 1% of each run, Pallas kernels for 21% -> 24%
where the time goes in v3:
time: 61 us; the launch traced here: 60.6 us
  starting transfers between devices  28.3 us (46%)
  Pallas kernels  16.3 us (27%)
  waiting for transfers between devices  14.6 us (24%)
  between operations  0.73 us (1%)
  other arithmetic  0.61 us (1%)
    ppermute x9, starting transfers between devices, shifted(): return lax.ppermute(x, axis, [(i, (i + step) % size) for i in range(size)])  14.2 us
    all_to_all x2, starting transfers between devices, all_to_all(): return lax.all_to_all(x, axes, split_axis=0, concat_axis=0, tiled=True)  13.5 us
    all_to_all x2, waiting for transfers between devices, all_to_all(): return lax.all_to_all(x, axes, split_axis=0, concat_axis=0, tiled=True)  9.2 us
    pallas_call x1, Pallas kernels, per_device(): pl.pallas_call(scatter_kernel, out_shape=[jax.ShapeDtypeStruct((quarter +...  5.72 us
    ppermute x9, waiting for transfers between devices, shifted(): return lax.ppermute(x, axis, [(i, (i + step) % size) for i in range(size)])  4.24 us
    pallas_call x1, Pallas kernels, per_device(): pl.pallas_call(near_kernel, out_shape=[jax.ShapeDtypeStruct((groups, LANE...  3.91 us
    pallas_call x1, Pallas kernels, per_device(): pl.pallas_call(prep_kernel, out_shape=[jax.ShapeDtypeStruct((2, groups, L...  2.49 us
    pallas_call x1, Pallas kernels, per_device(): pl.pallas_call(far_kernel, out_shape=[jax.ShapeDtypeStruct((groups, LANES...  2.29 us
  transfers between devices with their start and end apart: 14, of which 5 were waited for; matrix products, arithmetic and copies ran while one was open for 1% of the time, Pallas kernels for 24%

profile of v3, /device:TPU:2, one launch (start us, length us, event | category | flops | bytes accessed | tf_op | source)
XLA Modules:
  0.0 60.6 jit_solution(2528750260491004310)
XLA Ops:
  0.6 0.0 copy-start
  0.6 0.0 copy-start.3
  0.7 0.0 copy-start.2
  0.7 0.1 collective-permute-start.1
  0.8 2.5 %prep.1 = (f32[2,16,128]{2,1,0:T(8,128)}, bf16[8,64,256]{2,1,0:T(8,128)(2,1)}, bf16[8,64,256]{2,1,0:T(8,128)(2,1)}, bf16[8,64,256]{2,1,0:T(8,128)(2,1)}, bf16[8,64,256]{2,1,0:T(8,128)(2,1)}) custom-call(s32[16,128]{1,0:T(8,128)} %bitcast.13, f32[16,128]{1,0:T(8,128)} %bitcast.17, bf16[8,2,64,1024]{3,2,1,0:T(8,128)(2,1)} %bitcast.19), custom_call_target="tpu_custom_call" | custom-call | bytes 2097152 | tf_op jit(solution)/shard_map/prep/pallas_call | solution.py:306
  3.3 0.5 collective-permute-start
  3.8 1.5 %collective-permute-start.2 = (bf16[512,256]{1,0:T(8,128)(2,1)}, bf16[512,256]{1,0:T(8,128)(2,1)S(1)}, u32[]{:S(2)}, u32[]{:S(2)}) collective-permute-start(bf16[512,256]{1,0:T(8,128)(2,1)} %bitcast.22), channel_id=1, source_target_pairs={{0,1},{1,2},{2,3},{3,0},{4,5},{5,6},{6,7},{7,4},{8,9},{9,10},{10,1... | collective-permute-start | bytes 786440 | tf_op jit(solution)/shard_map/ppermute | solution.py:28
  5.3 0.0 copy-start.4
  5.3 0.0 copy-start.1
  5.3 0.8 %collective-permute-start.3 = (bf16[512,256]{1,0:T(8,128)(2,1)}, bf16[512,256]{1,0:T(8,128)(2,1)S(1)}, u32[]{:S(2)}, u32[]{:S(2)}) collective-permute-start(bf16[512,256]{1,0:T(8,128)(2,1)} %bitcast.21), channel_id=1, source_target_pairs={{0,3},{1,0},{2,1},{3,2},{4,7},{5,4},{6,5},{7,6},{8,11},{9,8},{10,9... | collective-permute-start | bytes 786440 | tf_op jit(solution)/shard_map/ppermute | solution.py:28
  6.0 0.0 collective-permute-done.oth_aux
  6.0 0.0 collective-permute-done.1.oth_docs
  6.0 0.0 copy-done
  6.0 0.0 copy-done.3
  6.1 0.0 copy-done.2
  6.1 5.7 %scatter.1 = (f32[528,256]{1,0:T(8,128)S(1)}, bf16[528,256]{1,0:T(8,128)(2,1)}, bf16[528,256]{1,0:T(8,128)(2,1)}, bf16[528,256]{1,0:T(8,128)(2,1)}) custom-call(s32[16,128]{1,0:T(8,128)S(1)} %bitcast.14, f32[16,128]{1,0:T(8,128)S(1)} %bitcast.18, bf16[2048,256]{1,0:T(8,128)(2,1)S(1)} %copy-done, f32[2,16,128]{2,1,0:T(8,128)S(1)} %collective-permute-done.oth_aux, ...), custom_call_target="tpu_custom_call" | custom-call | flops 4294967296 | bytes 3145728 | tf_op jit(solution)/shard_map/scatter/pallas_call | solution.py:329
  11.8 0.0 copy-done.4
  11.8 2.1 %collective-permute-start.4 = (bf16[512,256]{1,0:T(8,128)(2,1)S(1)}, bf16[512,256]{1,0:T(8,128)(2,1)S(1)}, u32[]{:S(2)}, u32[]{:S(2)}) collective-permute-start(bf16[512,256]{1,0:T(8,128)(2,1)S(1)} %bitcast.20), channel_id=1, source_target_pairs={{0,2},{1,3},{2,0},{3,1},{4,6},{5,7},{6,4},{7,5},{8,10},{9,11},{10,... | collective-permute-start | bytes 786440 | tf_op jit(solution)/shard_map/ppermute | solution.py:28
  13.9 0.0 collective-permute-done.2.rest_1_
  13.9 0.0 collective-permute-done.3.rest_2_
  13.9 0.0 copy-done.1
  13.9 3.9 %near.1 = (f32[16,128]{1,0:T(8,128)S(1)}, f32[16,128]{1,0:T(8,128)S(1)}, bf16[64,256]{1,0:T(8,128)(2,1)S(1)}) custom-call(s32[16,128]{1,0:T(8,128)S(1)} %bitcast.15, bf16[2048,256]{1,0:T(8,128)(2,1)S(1)} %copy-done, f32[2,16,128]{2,1,0:T(8,128)S(1)} %collective-permute-done.oth_aux, bf16[2048,256]{1,0:T(8,128)(2,1)S(1)} %collective-permute-done.1.oth_docs, ...), custom_call_target="tpu_custom_call" | custom-call | tf_op jit(solution)/shard_map/near/pallas_call | solution.py:342
  17.8 1.4 %collective-permute-start.9 = (bf16[528,256]{1,0:T(8,128)(2,1)}, bf16[528,256]{1,0:T(8,128)(2,1)S(1)}, u32[]{:S(2)}, u32[]{:S(2)}) collective-permute-start(bf16[528,256]{1,0:T(8,128)(2,1)} %get-tuple-element.50), channel_id=1, source_target_pairs={{0,64},{64,128},{128,192},{192,0},{1,65},{65,129},{129,193},{193,1... | collective-permute-start | bytes 811016 | tf_op jit(solution)/shard_map/ppermute | solution.py:28
  19.2 2.9 %collective-permute-start.10 = (bf16[528,256]{1,0:T(8,128)(2,1)}, bf16[528,256]{1,0:T(8,128)(2,1)S(1)}, u32[]{:S(2)}, u32[]{:S(2)}) collective-permute-start(bf16[528,256]{1,0:T(8,128)(2,1)} %get-tuple-element.51), channel_id=1, source_target_pairs={{0,128},{64,192},{128,0},{192,64},{1,129},{65,193},{129,1},{193,65... | collective-permute-start | bytes 811016 | tf_op jit(solution)/shard_map/ppermute | solution.py:28
  22.1 1.3 %collective-permute-start.11 = (bf16[528,256]{1,0:T(8,128)(2,1)}, bf16[528,256]{1,0:T(8,128)(2,1)S(1)}, u32[]{:S(2)}, u32[]{:S(2)}) collective-permute-start(bf16[528,256]{1,0:T(8,128)(2,1)} %get-tuple-element.52), channel_id=1, source_target_pairs={{0,192},{64,0},{128,64},{192,128},{1,193},{65,1},{129,65},{193,129... | collective-permute-start | bytes 811016 | tf_op jit(solution)/shard_map/ppermute | solution.py:28
  23.5 0.0 collective-permute-done.4.rest_0_
  23.5 2.3 %far.1 = (f32[16,128]{1,0:T(8,128)S(1)}, f32[16,128]{1,0:T(8,128)S(1)}, f32[32,1,128]{2,1,0:T(1,128)}, bf16[64,256]{1,0:T(8,128)(2,1)S(1)}) custom-call(s32[16,128]{1,0:T(8,128)S(1)} %bitcast.16, bf16[2048,256]{1,0:T(8,128)(2,1)S(1)} %copy-done, f32[2,16,128]{2,1,0:T(8,128)S(1)} %collective-permute-done.oth_aux, ...), custom_call_target="tpu_custom_call" | custom-call | tf_op jit(solution)/shard_map/far/pallas_call | solution.py:353
  25.8 6.2 %all-to-all-start = ((f32[32,1,128]{2,1,0:T(1,128)}), f32[32,1,128]{2,1,0:T(1,128)S(1)}, u32[]{:S(2)}, u32[]{:S(2)}) async-start(f32[32,1,128]{2,1,0:T(1,128)} %get-tuple-element.53), calls=%async_computation | async-start | bytes 32768 | tf_op jit(solution)/shard_map/all_to_all | solution.py:23
  32.0 0.0 collective-permute-done.9.refs_1_
  32.0 1.7 %collective-permute-done.10.refs_2_ = bf16[528,256]{1,0:T(8,128)(2,1)S(1)} collective-permute-done((bf16[528,256]{1,0:T(8,128)(2,1)}, bf16[528,256]{1,0:T(8,128)(2,1)S(1)}, u32[]{:S(2)}, u32[]{:S(2)}) %collective-permute-start.10) | collective-permute-done | bytes 270368 | tf_op jit(solution)/shard_map/ppermute | solution.py:28
  33.8 0.0 collective-permute-done.11.refs_3_
  33.8 4.3 %all-to-all-done.refs_4_ = f32[32,1,128]{2,1,0:T(1,128)S(1)} async-done(((f32[32,1,128]{2,1,0:T(1,128)}), f32[32,1,128]{2,1,0:T(1,128)S(1)}, u32[]{:S(2)}, u32[]{:S(2)}) %all-to-all-start) | async-done | bytes 16416 | tf_op jit(solution)/shard_map/all_to_all | solution.py:23
  38.0 1.1 %combine.1 = bf16[8,80,256]{2,1,0:T(8,128)(2,1)} custom-call(f32[528,256]{1,0:T(8,128)S(1)} %get-tuple-element.49.refs_0_, bf16[528,256]{1,0:T(8,128)(2,1)S(1)} %collective-permute-done.9.refs_1_, bf16[528,256]{1,0:T(8,128)(2,1)S(1)} %collective-permute-done.10.refs_2_, bf16[528,256]{1,0:T(8,128)(2,1)S(1)} %collective-permute-done.11.refs_3_, ...), custom_call_target="tpu_custom_call" | custom-call | bytes 1572864 | tf_op jit(solution)/shard_map/combine/pallas_call | solution.py:372
  39.1 7.3 %all-to-all-start.1 = ((bf16[8,80,256]{2,1,0:T(8,128)(2,1)}), bf16[8,80,256]{2,1,0:T(8,128)(2,1)S(1)}, u32[]{:S(2)}, u32[]{:S(2)}) async-start(bf16[8,80,256]{2,1,0:T(8,128)(2,1)} %combine.1), calls=%async_computation.1 | async-start | bytes 655360 | tf_op jit(solution)/shard_map/all_to_all | solution.py:23
  46.4 0.0 collective-permute-start.5
  46.4 1.2 %collective-permute-done.5 = f32[16,128]{1,0:T(8,128)S(1)} collective-permute-done((f32[16,128]{1,0:T(8,128)S(1)}, f32[16,128]{1,0:T(8,128)S(1)}, u32[]{:S(2)}, u32[]{:S(2)}) %collective-permute-start.5) | collective-permute-done | bytes 8224 | tf_op jit(solution)/shard_map/ppermute | solution.py:366
  47.6 1.5 %collective-permute-start.8 = (f32[16,128]{1,0:T(8,128)S(1)}, f32[16,128]{1,0:T(8,128)S(1)}, u32[]{:S(2)}, u32[]{:S(2)}) collective-permute-start(f32[16,128]{1,0:T(8,128)S(1)} %add.12), channel_id=1, source_target_pairs={{0,3},{1,0},{2,1},{3,2},{4,7},{5,4},{6,5},{7,6},{8,11},{9,8},{10,9... | collective-permute-start | bytes 24584 | tf_op jit(solution)/shard_map/ppermute | solution.py:28
  49.0 0.6 collective-permute-start.7
  49.6 2.1 %collective-permute-start.6 = (f32[16,128]{1,0:T(8,128)S(1)}, f32[16,128]{1,0:T(8,128)S(1)}, u32[]{:S(2)}, u32[]{:S(2)}) collective-permute-start(f32[16,128]{1,0:T(8,128)S(1)} %add.12), channel_id=1, source_target_pairs={{0,1},{1,2},{2,3},{3,0},{4,5},{5,6},{6,7},{7,4},{8,9},{9,10},{10,1... | collective-permute-start | bytes 24584 | tf_op jit(solution)/shard_map/ppermute | solution.py:28
  51.7 0.0 collective-permute-done.8
  51.7 2.5 %collective-permute-done.7 = f32[16,128]{1,0:T(8,128)S(1)} collective-permute-done((f32[16,128]{1,0:T(8,128)S(1)}, f32[16,128]{1,0:T(8,128)S(1)}, u32[]{:S(2)}, u32[]{:S(2)}) %collective-permute-start.7) | collective-permute-done | bytes 8224 | tf_op jit(solution)/shard_map/ppermute | solution.py:28
  54.2 0.0 collective-permute-done.6
  54.2 0.6 multiply_bitcast_fusion
  54.8 4.9 %all-to-all-done.1.recv = bf16[8,80,256]{2,1,0:T(8,128)(2,1)S(1)} async-done(((bf16[8,80,256]{2,1,0:T(8,128)(2,1)}), bf16[8,80,256]{2,1,0:T(8,128)(2,1)S(1)}, u32[]{:S(2)}, u32[]{:S(2)}) %all-to-all-start.1) | async-done | bytes 327712 | tf_op jit(solution)/shard_map/all_to_all | solution.py:23
  59.7 0.9 %update.1 = (bf16[64,256]{1,0:T(8,128)(2,1)}, f32[1,64]{1,0:T(1,128)}, f32[1,128]{1,0:T(1,128)}) custom-call(bf16[8,80,256]{2,1,0:T(8,128)(2,1)S(1)} %all-to-all-done.1.recv, bf16[64,256]{1,0:T(8,128)(2,1)S(1)} %get-tuple-element.54.old), custom_call_target="tpu_custom_call" | custom-call | bytes 294912 | tf_op jit(solution)/shard_map/update/pallas_call | solution.py:381
  (1 shorter events, 0.0 us)
Async XLA Ops:
  0.6 5.4 %copy-start = (bf16[2048,256]{1,0:T(8,128)(2,1)S(1)}, bf16[2048,256]{1,0:T(8,128)(2,1)}, u32[]{:S(2)}) copy-start(bf16[2048,256]{1,0:T(8,128)(2,1)} %own_docs.5) | copy-start | bytes 3145732
  0.6 5.4 %copy-start.3 = (f32[2048]{0:T(1024)S(1)}, f32[2048]{0:T(1024)}, u32[]{:S(2)}) copy-start(f32[2048]{0:T(1024)} %param.6) | copy-start | bytes 24580
  0.7 5.4 %copy-start.2 = (s32[2048]{0:T(1024)S(1)}, s32[2048]{0:T(1024)}, u32[]{:S(2)}) copy-start(s32[2048]{0:T(1024)} %param.5) | copy-start | bytes 24580
  0.7 5.4 %collective-permute-start.1 = (bf16[2048,256]{1,0:T(8,128)(2,1)}, bf16[2048,256]{1,0:T(8,128)(2,1)S(1)}, u32[]{:S(2)}, u32[]{:S(2)}) collective-permute-start(bf16[2048,256]{1,0:T(8,128)(2,1)} %own_docs.5), channel_id=1, source_target_pairs={{0,4},{4,0},{1,5},{5,1},{2,6},{6,2},{3,7},{7,3},{8,12},{12,8},{9,1... | collective-permute-start | bytes 3145736 | tf_op jit(solution)/shard_map/ppermute | solution.py:302
  3.3 2.8 %collective-permute-start = (f32[2,16,128]{2,1,0:T(8,128)}, f32[2,16,128]{2,1,0:T(8,128)S(1)}, u32[]{:S(2)}, u32[]{:S(2)}) collective-permute-start(f32[2,16,128]{2,1,0:T(8,128)} %get-tuple-element.31), channel_id=1, source_target_pairs={{0,4},{4,0},{1,5},{5,1},{2,6},{6,2},{3,7},{7,3},{8,12},{12,8},{9,1... | collective-permute-start | bytes 49160 | tf_op jit(solution)/shard_map/ppermute | solution.py:325
  3.8 10.1 %collective-permute-start.2 = (bf16[512,256]{1,0:T(8,128)(2,1)}, bf16[512,256]{1,0:T(8,128)(2,1)S(1)}, u32[]{:S(2)}, u32[]{:S(2)}) collective-permute-start(bf16[512,256]{1,0:T(8,128)(2,1)} %bitcast.22), channel_id=1, source_target_pairs={{0,1},{1,2},{2,3},{3,0},{4,5},{5,6},{6,7},{7,4},{8,9},{9,10},{10,1... | collective-permute-start | bytes 786440 | tf_op jit(solution)/shard_map/ppermute | solution.py:28
  5.3 6.5 %copy-start.4 = (bf16[8,64,256]{2,1,0:T(8,128)(2,1)S(1)}, bf16[8,64,256]{2,1,0:T(8,128)(2,1)}, u32[]{:S(2)}) copy-start(bf16[8,64,256]{2,1,0:T(8,128)(2,1)} %get-tuple-element.45) | copy-start | bytes 786436
  5.3 8.6 %copy-start.1 = (bf16[8,64,256]{2,1,0:T(8,128)(2,1)S(1)}, bf16[8,64,256]{2,1,0:T(8,128)(2,1)}, u32[]{:S(2)}) copy-start(bf16[8,64,256]{2,1,0:T(8,128)(2,1)} %get-tuple-element.36) | copy-start | bytes 786436
  5.3 8.6 %collective-permute-start.3 = (bf16[512,256]{1,0:T(8,128)(2,1)}, bf16[512,256]{1,0:T(8,128)(2,1)S(1)}, u32[]{:S(2)}, u32[]{:S(2)}) collective-permute-start(bf16[512,256]{1,0:T(8,128)(2,1)} %bitcast.21), channel_id=1, source_target_pairs={{0,3},{1,0},{2,1},{3,2},{4,7},{5,4},{6,5},{7,6},{8,11},{9,8},{10,9... | collective-permute-start | bytes 786440 | tf_op jit(solution)/shard_map/ppermute | solution.py:28
  11.8 11.7 %collective-permute-start.4 = (bf16[512,256]{1,0:T(8,128)(2,1)S(1)}, bf16[512,256]{1,0:T(8,128)(2,1)S(1)}, u32[]{:S(2)}, u32[]{:S(2)}) collective-permute-start(bf16[512,256]{1,0:T(8,128)(2,1)S(1)} %bitcast.20), channel_id=1, source_target_pairs={{0,2},{1,3},{2,0},{3,1},{4,6},{5,7},{6,4},{7,5},{8,10},{9,11},{10,... | collective-permute-start | bytes 786440 | tf_op jit(solution)/shard_map/ppermute | solution.py:28
  17.8 14.2 %collective-permute-start.9 = (bf16[528,256]{1,0:T(8,128)(2,1)}, bf16[528,256]{1,0:T(8,128)(2,1)S(1)}, u32[]{:S(2)}, u32[]{:S(2)}) collective-permute-start(bf16[528,256]{1,0:T(8,128)(2,1)} %get-tuple-element.50), channel_id=1, source_target_pairs={{0,64},{64,128},{128,192},{192,0},{1,65},{65,129},{129,193},{193,1... | collective-permute-start | bytes 811016 | tf_op jit(solution)/shard_map/ppermute | solution.py:28
  19.2 14.5 %collective-permute-start.10 = (bf16[528,256]{1,0:T(8,128)(2,1)}, bf16[528,256]{1,0:T(8,128)(2,1)S(1)}, u32[]{:S(2)}, u32[]{:S(2)}) collective-permute-start(bf16[528,256]{1,0:T(8,128)(2,1)} %get-tuple-element.51), channel_id=1, source_target_pairs={{0,128},{64,192},{128,0},{192,64},{1,129},{65,193},{129,1},{193,65... | collective-permute-start | bytes 811016 | tf_op jit(solution)/shard_map/ppermute | solution.py:28
  22.1 11.6 %collective-permute-start.11 = (bf16[528,256]{1,0:T(8,128)(2,1)}, bf16[528,256]{1,0:T(8,128)(2,1)S(1)}, u32[]{:S(2)}, u32[]{:S(2)}) collective-permute-start(bf16[528,256]{1,0:T(8,128)(2,1)} %get-tuple-element.52), channel_id=1, source_target_pairs={{0,192},{64,0},{128,64},{192,128},{1,193},{65,1},{129,65},{193,129... | collective-permute-start | bytes 811016 | tf_op jit(solution)/shard_map/ppermute | solution.py:28
  25.8 12.3 %all-to-all-start = ((f32[32,1,128]{2,1,0:T(1,128)}), f32[32,1,128]{2,1,0:T(1,128)S(1)}, u32[]{:S(2)}, u32[]{:S(2)}) async-start(f32[32,1,128]{2,1,0:T(1,128)} %get-tuple-element.53), calls=%async_computation | async-start | bytes 32768 | tf_op jit(solution)/shard_map/all_to_all | solution.py:23
  39.1 20.6 %all-to-all-start.1 = ((bf16[8,80,256]{2,1,0:T(8,128)(2,1)}), bf16[8,80,256]{2,1,0:T(8,128)(2,1)S(1)}, u32[]{:S(2)}, u32[]{:S(2)}) async-start(bf16[8,80,256]{2,1,0:T(8,128)(2,1)} %combine.1), calls=%async_computation.1 | async-start | bytes 655360 | tf_op jit(solution)/shard_map/all_to_all | solution.py:23
  46.4 1.2 %collective-permute-start.5 = (f32[16,128]{1,0:T(8,128)S(1)}, f32[16,128]{1,0:T(8,128)S(1)}, u32[]{:S(2)}, u32[]{:S(2)}) collective-permute-start(f32[16,128]{1,0:T(8,128)S(1)} %get-tuple-element.48), channel_id=1, source_target_pairs={{0,4},{4,0},{1,5},{5,1},{2,6},{6,2},{3,7},{7,3},{8,12},{12,8},{9,1... | collective-permute-start | bytes 24584 | tf_op jit(solution)/shard_map/ppermute | solution.py:366
  47.6 4.1 %collective-permute-start.8 = (f32[16,128]{1,0:T(8,128)S(1)}, f32[16,128]{1,0:T(8,128)S(1)}, u32[]{:S(2)}, u32[]{:S(2)}) collective-permute-start(f32[16,128]{1,0:T(8,128)S(1)} %add.12), channel_id=1, source_target_pairs={{0,3},{1,0},{2,1},{3,2},{4,7},{5,4},{6,5},{7,6},{8,11},{9,8},{10,9... | collective-permute-start | bytes 24584 | tf_op jit(solution)/shard_map/ppermute | solution.py:28
  49.0 5.2 %collective-permute-start.7 = (f32[16,128]{1,0:T(8,128)S(1)}, f32[16,128]{1,0:T(8,128)S(1)}, u32[]{:S(2)}, u32[]{:S(2)}) collective-permute-start(f32[16,128]{1,0:T(8,128)S(1)} %add.12), channel_id=1, source_target_pairs={{0,2},{1,3},{2,0},{3,1},{4,6},{5,7},{6,4},{7,5},{8,10},{9,11},{10,... | collective-permute-start | bytes 24584 | tf_op jit(solution)/shard_map/ppermute | solution.py:28
  49.6 4.6 %collective-permute-start.6 = (f32[16,128]{1,0:T(8,128)S(1)}, f32[16,128]{1,0:T(8,128)S(1)}, u32[]{:S(2)}, u32[]{:S(2)}) collective-permute-start(f32[16,128]{1,0:T(8,128)S(1)} %add.12), channel_id=1, source_target_pairs={{0,1},{1,2},{2,3},{3,0},{4,5},{5,6},{6,7},{7,4},{8,9},{9,10},{10,1... | collective-permute-start | bytes 24584 | tf_op jit(solution)/shard_map/ppermute | solution.py:28
